TPU v7x, 32 devices: a whole 2x2x4 slice. The times are simulated.
32 devices in a mesh: starts: 2 (over y), gx: 8 (over z, x), gy: 2 (over core).
Axes of the slice: x: 2, y: 2, z: 4, core: 2. Of those that a mesh axis runs over, the one named last changes fastest.
Arguments:
- chi_final: float32 [2, 64, 128, 256], P(None, ('starts', 'gx'), 'gy'), parts along dimension 1, may hold values from -30 to 30
- psi_late: float32 [2, 64, 128, 256], P(None, ('starts', 'gx'), 'gy'), parts along dimension 1, may hold values from -0.7 to 0.7
- psi_early: float32 [2, 64, 128, 256], P(None, ('starts', 'gx'), 'gy'), parts along dimension 1, may hold values from -0.7 to 0.7
- trap: float32 [32, 128, 256], P('gx', 'gy'), may hold values from 0 to 1
- controls: float32 [4, 64, 256], P('starts', 'gy'), parts along dimension 0, may hold values from -0.5 to 0.5
Outputs:
- chi_start: float32 [2, 64, 128, 256], P(None, ('starts', 'gx'), 'gy'), parts along dimension 1
- grad_rows: float32 [4, 64, 256], P('starts', 'gy'), parts along dimension 0
- adjoint_power: float32 [2], P('starts'), parts along dimension 0
There are 2 independent parts, one for each index of `starts`. A program takes and returns all parts, laid end to end along the dimension named above; an argument that names none is the same for every part. Nothing has to cross between parts.
All inputs are finite; a program needn't handle non-finite values.
Results may differ from a plain program's by a relative error of at most 0.0005.
Values sent between devices are 32-bit elements; how exact they have to be, the bound alone decides.
A program may use at most 64 MiB of HBM per device.

v0:
```python
import math

import jax
import jax.numpy as jnp
from jax import lax
from jax.sharding import PartitionSpec as P

COUPLING = 1.0
STEP_SIZE = 0.2


def extended(block, sides, width):
    for axis, dim in sides:
        count = lax.axis_size(axis)
        forward = [(i, i + 1) for i in range(count - 1)]
        backward = [(target, source) for source, target in forward]
        low = lax.ppermute(
            lax.slice_in_dim(block, block.shape[dim] - width, None, axis=dim), axis, forward
        )
        high = lax.ppermute(lax.slice_in_dim(block, 0, width, axis=dim), axis, backward)
        block = jnp.concatenate([low, block, high], axis=dim)
    return block


def coefficients(psi, trap, control, profile):
    real_part = psi[0]
    imag_part = psi[1]
    fine_control = jnp.repeat(control, 2, axis=0)
    potential = trap + profile[:, None, None] * fine_control[None, :, :]
    weight = potential + 2.0 * COUPLING * (real_part * real_part + imag_part * imag_part)
    mix_a = COUPLING * (real_part * real_part - imag_part * imag_part)
    mix_b = 2.0 * COUPLING * real_part * imag_part
    return (weight, mix_a, mix_b)


def apply_coef(lapl, field, coef):
    weight, mix_a, mix_b = coef
    real_part = field[0]
    imag_part = field[1]
    upper = -0.5 * lapl[0] + (weight + mix_a) * real_part + mix_b * imag_part
    lower = -0.5 * lapl[1] + mix_b * real_part + (weight - mix_a) * imag_part
    return jnp.stack([-lower, upper])


def operator(field, coef):
    padded = extended(field, (("gx", 1), ("gy", 2)), 1)
    z_padded = jnp.pad(field, ((0, 0), (0, 0), (0, 0), (1, 1)))
    total = padded[:, 2:, 1:-1, :] + padded[:, :-2, 1:-1, :]
    total = total + padded[:, 1:-1, 2:, :] + padded[:, 1:-1, :-2, :]
    total = total + z_padded[:, :, :, 2:] + z_padded[:, :, :, :-2]
    lapl = total - 6.0 * field
    return apply_coef(lapl, field, coef)


def rk_step(field, coef):
    section_one = operator(field, coef)
    section_two = operator(field + 0.5 * STEP_SIZE * section_one, coef)
    section_three = operator(field + 0.5 * STEP_SIZE * section_two, coef)
    section_four = operator(field + STEP_SIZE * section_three, coef)
    return field + STEP_SIZE / 6.0 * (
        section_one + 2.0 * section_two + 2.0 * section_three + section_four
    )


def row_terms(field, psi, profile):
    intersection = field[0] * psi[1] - field[1] * psi[0]
    summed = jnp.sum(intersection * profile[:, None, None], axis=0)
    return summed.reshape(summed.shape[0] // 2, 2, summed.shape[1]).sum(axis=1)


def on_device(chi_final, psi_late, psi_early, trap, controls):
    planes = chi_final.shape[1]
    width_y = chi_final.shape[2]
    depth = chi_final.shape[3]
    total_x = planes * lax.axis_size("gx")
    total_y = width_y * lax.axis_size("gy")
    first = lax.axis_index("gx") * planes
    x_index = (first + jnp.arange(planes, dtype=jnp.int32)).astype(jnp.float32)
    profile = 1.0 + 0.5 * jnp.cos(2.0 * math.pi * x_index / float(total_x))
    coef_late = coefficients(psi_late, trap, controls[1], profile)
    coef_early = coefficients(psi_early, trap, controls[0], profile)
    chi_late = rk_step(chi_final, coef_late)
    chi_start = rk_step(chi_late, coef_early)
    rows = jnp.stack(
        [row_terms(chi_start, psi_early, profile), row_terms(chi_late, psi_late, profile)]
    )
    local_sq = jnp.sum(chi_start * chi_start)
    squares = lax.psum(local_sq, ("gx", "gy"))
    rows_sum = lax.psum(rows, "gx")
    power = squares / float(total_x * total_y * depth)
    grad_rows = rows_sum / jnp.sqrt(float(total_x) * (power + 1e-06))
    return (chi_start, grad_rows, jnp.reshape(power, (1,)))


def solution(mesh):
    placed = (
        P(None, ("starts", "gx"), "gy", None),
        P(None, ("starts", "gx"), "gy", None),
        P(None, ("starts", "gx"), "gy", None),
        P("gx", "gy", None),
        P("starts", "gy", None),
    )
    return jax.shard_map(
        on_device,
        mesh=mesh,
        in_specs=placed,
        out_specs=(P(None, ("starts", "gx"), "gy", None), P("starts", "gy", None), P("starts")),
        check_vma=False,
    )
```

profile of v0, /device:TPU:0, one launch (start us, length us, event | category | flops | bytes accessed | tf_op | source)
XLA Modules:
  0.0 232.0 jit_solution(15009674649921705698)
XLA Ops:
  7.2 1.0 fusion.145
  8.3 1.3 collective-permute-start
  9.6 5.5 %collective-permute-start.1 = (f32[2,1,64,256]{3,2,1,0:T(8,128)S(1)}, f32[2,1,64,256]{3,2,1,0:T(8,128)S(1)}, u32[]{:S(2)}, u32[]{:S(2)}) collective-permute-start(f32[2,1,64,256]{3,2,1,0:T(8,128)S(1)} %get-tuple-element.62), channel_id=1, source_target_pairs={{0,2},{2,4},{4,6},{6,8},{8,10},{10,12},{12,14},{1,3},{3,5},{5,7},{... | collective-permute-start | bytes 393224 | tf_op jit(solution)/shard_map/ppermute | solution.py:17
  15.1 1.4 slice_bitcast_fusion.14
  16.4 3.1 %collective-permute-done.1 = f32[2,1,64,256]{3,2,1,0:T(8,128)S(1)} collective-permute-done((f32[2,1,64,256]{3,2,1,0:T(8,128)S(1)}, f32[2,1,64,256]{3,2,1,0:T(8,128)S(1)}, u32[]{:S(2)}, u32[]{:S(2)}) %collective-permute-start.1) | collective-permute-done | bytes 131104 | tf_op jit(solution)/shard_map/ppermute | solution.py:17
  19.7 1.3 collective-permute-start.2
  21.0 3.0 %collective-permute-start.3 = (f32[2,6,1,256]{3,2,1,0:T(1,128)S(1)}, f32[2,6,1,256]{3,2,1,0:T(1,128)S(1)}, u32[]{:S(2)}, u32[]{:S(2)}) collective-permute-start(f32[2,6,1,256]{3,2,1,0:T(1,128)S(1)} %get-tuple-element.46), channel_id=1, source_target_pairs={{0,1},{2,3},{4,5},{6,7},{8,9},{10,11},{12,13},{14,15},{16,17},{18,... | collective-permute-start | bytes 36872 | tf_op jit(solution)/shard_map/ppermute | solution.py:17
  24.2 0.6 collective-permute-done.3
  25.7 4.4 %collective-permute-start.5 = (f32[2,1,64,256]{3,2,1,0:T(8,128)S(1)}, f32[2,1,64,256]{3,2,1,0:T(8,128)S(1)}, u32[]{:S(2)}, u32[]{:S(2)}) collective-permute-start(f32[2,1,64,256]{3,2,1,0:T(8,128)S(1)} %get-tuple-element.59), channel_id=1, source_target_pairs={{0,2},{2,4},{4,6},{6,8},{8,10},{10,12},{12,14},{1,3},{3,5},{5,7},{... | collective-permute-start | bytes 393224 | tf_op jit(solution)/shard_map/ppermute | solution.py:17
  30.1 1.3 collective-permute-start.4
  31.4 1.9 collective-permute-done.5
  33.3 4.1 %collective-permute-done.4 = f32[2,1,64,256]{3,2,1,0:T(8,128)S(1)} collective-permute-done((f32[2,1,64,256]{3,2,1,0:T(8,128)S(1)}, f32[2,1,64,256]{3,2,1,0:T(8,128)S(1)}, u32[]{:S(2)}, u32[]{:S(2)}) %collective-permute-start.4) | collective-permute-done | bytes 131104 | tf_op jit(solution)/shard_map/ppermute | solution.py:20
  37.5 1.3 collective-permute-start.6
  38.8 3.0 %collective-permute-start.7 = (f32[2,6,1,256]{3,2,1,0:T(1,128)S(1)}, f32[2,6,1,256]{3,2,1,0:T(1,128)S(1)}, u32[]{:S(2)}, u32[]{:S(2)}) collective-permute-start(f32[2,6,1,256]{3,2,1,0:T(1,128)S(1)} %get-tuple-element.44), channel_id=1, source_target_pairs={{0,1},{2,3},{4,5},{6,7},{8,9},{10,11},{12,13},{14,15},{16,17},{18,... | collective-permute-start | bytes 36872 | tf_op jit(solution)/shard_map/ppermute | solution.py:17
  41.8 0.8 collective-permute-done.7
  43.3 4.5 %collective-permute-start.9 = (f32[2,1,64,256]{3,2,1,0:T(8,128)S(1)}, f32[2,1,64,256]{3,2,1,0:T(8,128)S(1)}, u32[]{:S(2)}, u32[]{:S(2)}) collective-permute-start(f32[2,1,64,256]{3,2,1,0:T(8,128)S(1)} %get-tuple-element.57), channel_id=1, source_target_pairs={{0,2},{2,4},{4,6},{6,8},{8,10},{10,12},{12,14},{1,3},{3,5},{5,7},{... | collective-permute-start | bytes 393224 | tf_op jit(solution)/shard_map/ppermute | solution.py:17
  47.8 1.3 collective-permute-start.8
  49.1 1.9 collective-permute-done.9
  51.1 4.1 %collective-permute-done.8 = f32[2,1,64,256]{3,2,1,0:T(8,128)S(1)} collective-permute-done((f32[2,1,64,256]{3,2,1,0:T(8,128)S(1)}, f32[2,1,64,256]{3,2,1,0:T(8,128)S(1)}, u32[]{:S(2)}, u32[]{:S(2)}) %collective-permute-start.8) | collective-permute-done | bytes 131104 | tf_op jit(solution)/shard_map/ppermute | solution.py:20
  55.2 1.3 collective-permute-start.10
  56.5 3.0 %collective-permute-start.11 = (f32[2,6,1,256]{3,2,1,0:T(1,128)S(1)}, f32[2,6,1,256]{3,2,1,0:T(1,128)S(1)}, u32[]{:S(2)}, u32[]{:S(2)}) collective-permute-start(f32[2,6,1,256]{3,2,1,0:T(1,128)S(1)} %get-tuple-element.42), channel_id=1, source_target_pairs={{0,1},{2,3},{4,5},{6,7},{8,9},{10,11},{12,13},{14,15},{16,17},{18,... | collective-permute-start | bytes 36872 | tf_op jit(solution)/shard_map/ppermute | solution.py:17
  59.6 0.8 collective-permute-done.11
  61.0 4.0 %collective-permute-start.13 = (f32[2,1,64,256]{3,2,1,0:T(8,128)S(1)}, f32[2,1,64,256]{3,2,1,0:T(8,128)S(1)}, u32[]{:S(2)}, u32[]{:S(2)}) collective-permute-start(f32[2,1,64,256]{3,2,1,0:T(8,128)S(1)} %get-tuple-element.55), channel_id=1, source_target_pairs={{0,2},{2,4},{4,6},{6,8},{8,10},{10,12},{12,14},{1,3},{3,5},{5,7},{... | collective-permute-start | bytes 393224 | tf_op jit(solution)/shard_map/ppermute | solution.py:17
  65.0 1.3 collective-permute-start.12
  66.3 1.9 collective-permute-done.13
  68.2 4.1 %collective-permute-done.12 = f32[2,1,64,256]{3,2,1,0:T(8,128)S(1)} collective-permute-done((f32[2,1,64,256]{3,2,1,0:T(8,128)S(1)}, f32[2,1,64,256]{3,2,1,0:T(8,128)S(1)}, u32[]{:S(2)}, u32[]{:S(2)}) %collective-permute-start.12) | collective-permute-done | bytes 131104 | tf_op jit(solution)/shard_map/ppermute | solution.py:20
  72.4 1.3 collective-permute-start.14
  73.7 3.0 %collective-permute-start.15 = (f32[2,6,1,256]{3,2,1,0:T(1,128)S(1)}, f32[2,6,1,256]{3,2,1,0:T(1,128)S(1)}, u32[]{:S(2)}, u32[]{:S(2)}) collective-permute-start(f32[2,6,1,256]{3,2,1,0:T(1,128)S(1)} %get-tuple-element.40), channel_id=1, source_target_pairs={{0,1},{2,3},{4,5},{6,7},{8,9},{10,11},{12,13},{14,15},{16,17},{18,... | collective-permute-start | bytes 36872 | tf_op jit(solution)/shard_map/ppermute | solution.py:17
  76.7 0.8 collective-permute-done.15
  78.2 4.0 %collective-permute-start.17 = (f32[2,1,64,256]{3,2,1,0:T(8,128)S(1)}, f32[2,1,64,256]{3,2,1,0:T(8,128)S(1)}, u32[]{:S(2)}, u32[]{:S(2)}) collective-permute-start(f32[2,1,64,256]{3,2,1,0:T(8,128)S(1)} %get-tuple-element.53), channel_id=1, source_target_pairs={{0,2},{2,4},{4,6},{6,8},{8,10},{10,12},{12,14},{1,3},{3,5},{5,7},{... | collective-permute-start | bytes 393224 | tf_op jit(solution)/shard_map/ppermute | solution.py:17
  82.2 1.3 collective-permute-start.16
  83.5 1.9 collective-permute-done.17
  85.5 4.1 %collective-permute-done.16 = f32[2,1,64,256]{3,2,1,0:T(8,128)S(1)} collective-permute-done((f32[2,1,64,256]{3,2,1,0:T(8,128)S(1)}, f32[2,1,64,256]{3,2,1,0:T(8,128)S(1)}, u32[]{:S(2)}, u32[]{:S(2)}) %collective-permute-start.16) | collective-permute-done | bytes 131104 | tf_op jit(solution)/shard_map/ppermute | solution.py:20
  89.6 0.6 pad_maximum_fusion.78
  90.2 1.3 collective-permute-start.18
  91.5 4.2 %collective-permute-start.19 = (f32[2,6,1,256]{3,2,1,0:T(1,128)S(1)}, f32[2,6,1,256]{3,2,1,0:T(1,128)}, u32[]{:S(2)}, u32[]{:S(2)}) collective-permute-start(f32[2,6,1,256]{3,2,1,0:T(1,128)S(1)} %get-tuple-element.38), channel_id=1, source_target_pairs={{0,1},{2,3},{4,5},{6,7},{8,9},{10,11},{12,13},{14,15},{16,17},{18,... | collective-permute-start | bytes 36872 | tf_op jit(solution)/shard_map/ppermute | solution.py:17
  95.7 0.7 broadcast_in_dim.5
  96.4 1.5 mul.427
  97.9 1.3 fusion.14
  99.9 4.0 %collective-permute-start.21 = (f32[2,1,64,256]{3,2,1,0:T(8,128)S(1)}, f32[2,1,64,256]{3,2,1,0:T(8,128)S(1)}, u32[]{:S(2)}, u32[]{:S(2)}) collective-permute-start(f32[2,1,64,256]{3,2,1,0:T(8,128)S(1)} %get-tuple-element.51), channel_id=1, source_target_pairs={{0,2},{2,4},{4,6},{6,8},{8,10},{10,12},{12,14},{1,3},{3,5},{5,7},{... | collective-permute-start | bytes 393224 | tf_op jit(solution)/shard_map/ppermute | solution.py:17
  103.9 1.3 collective-permute-start.20
  105.2 1.2 collective-permute-done.21
  106.4 4.4 %collective-permute-done.20 = f32[2,1,64,256]{3,2,1,0:T(8,128)S(1)} collective-permute-done((f32[2,1,64,256]{3,2,1,0:T(8,128)S(1)}, f32[2,1,64,256]{3,2,1,0:T(8,128)S(1)}, u32[]{:S(2)}, u32[]{:S(2)}) %collective-permute-start.20) | collective-permute-done | bytes 131104 | tf_op jit(solution)/shard_map/ppermute | solution.py:20
  110.8 1.3 collective-permute-start.22
  112.1 3.0 %collective-permute-start.23 = (f32[2,6,1,256]{3,2,1,0:T(1,128)S(1)}, f32[2,6,1,256]{3,2,1,0:T(1,128)S(1)}, u32[]{:S(2)}, u32[]{:S(2)}) collective-permute-start(f32[2,6,1,256]{3,2,1,0:T(1,128)S(1)} %get-tuple-element.36), channel_id=1, source_target_pairs={{0,1},{2,3},{4,5},{6,7},{8,9},{10,11},{12,13},{14,15},{16,17},{18,... | collective-permute-start | bytes 36872 | tf_op jit(solution)/shard_map/ppermute | solution.py:17
  115.1 0.8 collective-permute-done.23
  116.7 4.0 %collective-permute-start.25 = (f32[2,1,64,256]{3,2,1,0:T(8,128)S(1)}, f32[2,1,64,256]{3,2,1,0:T(8,128)S(1)}, u32[]{:S(2)}, u32[]{:S(2)}) collective-permute-start(f32[2,1,64,256]{3,2,1,0:T(8,128)S(1)} %get-tuple-element.49), channel_id=1, source_target_pairs={{0,2},{2,4},{4,6},{6,8},{8,10},{10,12},{12,14},{1,3},{3,5},{5,7},{... | collective-permute-start | bytes 393224 | tf_op jit(solution)/shard_map/ppermute | solution.py:17
  120.7 1.3 collective-permute-start.24
  122.0 1.9 collective-permute-done.25
  124.0 4.1 %collective-permute-done.24 = f32[2,1,64,256]{3,2,1,0:T(8,128)S(1)} collective-permute-done((f32[2,1,64,256]{3,2,1,0:T(8,128)S(1)}, f32[2,1,64,256]{3,2,1,0:T(8,128)S(1)}, u32[]{:S(2)}, u32[]{:S(2)}) %collective-permute-start.24) | collective-permute-done | bytes 131104 | tf_op jit(solution)/shard_map/ppermute | solution.py:20
  128.1 1.3 collective-permute-start.26
  129.4 3.0 %collective-permute-start.27 = (f32[2,6,1,256]{3,2,1,0:T(1,128)S(1)}, f32[2,6,1,256]{3,2,1,0:T(1,128)S(1)}, u32[]{:S(2)}, u32[]{:S(2)}) collective-permute-start(f32[2,6,1,256]{3,2,1,0:T(1,128)S(1)} %get-tuple-element.34), channel_id=1, source_target_pairs={{0,1},{2,3},{4,5},{6,7},{8,9},{10,11},{12,13},{14,15},{16,17},{18,... | collective-permute-start | bytes 36872 | tf_op jit(solution)/shard_map/ppermute | solution.py:17
  132.5 0.8 collective-permute-done.27
  134.1 3.8 %collective-permute-start.29 = (f32[2,1,64,256]{3,2,1,0:T(8,128)S(1)}, f32[2,1,64,256]{3,2,1,0:T(8,128)S(1)}, u32[]{:S(2)}, u32[]{:S(2)}) collective-permute-start(f32[2,1,64,256]{3,2,1,0:T(8,128)S(1)} %get-tuple-element.47), channel_id=1, source_target_pairs={{0,2},{2,4},{4,6},{6,8},{8,10},{10,12},{12,14},{1,3},{3,5},{5,7},{... | collective-permute-start | bytes 393224 | tf_op jit(solution)/shard_map/ppermute | solution.py:17
  137.8 1.3 collective-permute-start.28
  139.1 1.9 collective-permute-done.29
  141.1 4.1 %collective-permute-done.28 = f32[2,1,64,256]{3,2,1,0:T(8,128)S(1)} collective-permute-done((f32[2,1,64,256]{3,2,1,0:T(8,128)S(1)}, f32[2,1,64,256]{3,2,1,0:T(8,128)S(1)}, u32[]{:S(2)}, u32[]{:S(2)}) %collective-permute-start.28) | collective-permute-done | bytes 131104 | tf_op jit(solution)/shard_map/ppermute | solution.py:20
  145.2 1.3 collective-permute-start.30
  146.5 3.0 %collective-permute-start.31 = (f32[2,6,1,256]{3,2,1,0:T(1,128)S(1)}, f32[2,6,1,256]{3,2,1,0:T(1,128)S(1)}, u32[]{:S(2)}, u32[]{:S(2)}) collective-permute-start(f32[2,6,1,256]{3,2,1,0:T(1,128)S(1)} %get-tuple-element.32), channel_id=1, source_target_pairs={{0,1},{2,3},{4,5},{6,7},{8,9},{10,11},{12,13},{14,15},{16,17},{18,... | collective-permute-start | bytes 36872 | tf_op jit(solution)/shard_map/ppermute | solution.py:17
  149.6 0.8 collective-permute-done.31
  150.9 1.1 multiply_reduce_fusion
  153.7 32.2 %psum.15 = f32[]{:T(128)} all-reduce(f32[]{:T(128)} %get-tuple-element.5), channel_id=1, replica_groups=mesh['starts'=2,'gx'=8,'gy'=2] {'gx','gy'}, use_global_device_ids=true, to_apply=%region_6.7 | all-reduce | flops 1 | bytes 8 | tf_op jit(solution)/shard_map/psum | solution.py:88
  186.6 35.9 %all-reduce.10.cloned.1.call-done = f32[2,32,256]{2,1,0:T(8,128)} async-done(((f32[2,32,256]{2,1,0:T(8,128)}), f32[2,32,256]{2,1,0:T(8,128)}) %all-reduce.10.cloned.1.call-update) | async-done | bytes 65552 | tf_op jit(solution)/shard_map/psum | solution.py:89
  222.5 1.5 broadcast_divide_fusion
  (80 shorter events, 7.5 us)
Async XLA Ops:
  7.2 12.4 %copy-start = (f32[2,4,64,256]{3,2,1,0:T(8,128)S(1)}, f32[2,4,64,256]{3,2,1,0:T(8,128)}, u32[]{:S(2)}) copy-start(f32[2,4,64,256]{3,2,1,0:T(8,128)} %param.5) | copy-start | bytes 1572868
  7.2 215.3 %all-reduce.10.cloned.1.call-start = ((), (), s32[]{:S(2)}) async-start(), calls=%async_computation | async-start | bytes 131072 | tf_op jit(solution)/shard_map/psum | solution.py:89
  8.3 11.4 %collective-permute-start = (f32[2,1,64,256]{3,2,1,0:T(8,128)S(1)}, f32[2,1,64,256]{3,2,1,0:T(8,128)S(1)}, u32[]{:S(2)}, u32[]{:S(2)}) collective-permute-start(f32[2,1,64,256]{3,2,1,0:T(8,128)S(1)} %get-tuple-element.61), channel_id=1, source_target_pairs={{2,0},{4,2},{6,4},{8,6},{10,8},{12,10},{14,12},{3,1},{5,3},{7,5},{... | collective-permute-start | bytes 393224 | tf_op jit(solution)/shard_map/ppermute | solution.py:20
  9.6 10.0 %collective-permute-start.1 = (f32[2,1,64,256]{3,2,1,0:T(8,128)S(1)}, f32[2,1,64,256]{3,2,1,0:T(8,128)S(1)}, u32[]{:S(2)}, u32[]{:S(2)}) collective-permute-start(f32[2,1,64,256]{3,2,1,0:T(8,128)S(1)} %get-tuple-element.62), channel_id=1, source_target_pairs={{0,2},{2,4},{4,6},{6,8},{8,10},{10,12},{12,14},{1,3},{3,5},{5,7},{... | collective-permute-start | bytes 393224 | tf_op jit(solution)/shard_map/ppermute | solution.py:17
  19.7 4.5 %collective-permute-start.2 = (f32[2,6,1,256]{3,2,1,0:T(1,128)S(1)}, f32[2,6,1,256]{3,2,1,0:T(1,128)S(1)}, u32[]{:S(2)}, u32[]{:S(2)}) collective-permute-start(f32[2,6,1,256]{3,2,1,0:T(1,128)S(1)} %get-tuple-element.45), channel_id=1, source_target_pairs={{1,0},{3,2},{5,4},{7,6},{9,8},{11,10},{13,12},{15,14},{17,16},{19,... | collective-permute-start | bytes 36872 | tf_op jit(solution)/shard_map/ppermute | solution.py:20
  21.0 3.9 %collective-permute-start.3 = (f32[2,6,1,256]{3,2,1,0:T(1,128)S(1)}, f32[2,6,1,256]{3,2,1,0:T(1,128)S(1)}, u32[]{:S(2)}, u32[]{:S(2)}) collective-permute-start(f32[2,6,1,256]{3,2,1,0:T(1,128)S(1)} %get-tuple-element.46), channel_id=1, source_target_pairs={{0,1},{2,3},{4,5},{6,7},{8,9},{10,11},{12,13},{14,15},{16,17},{18,... | collective-permute-start | bytes 36872 | tf_op jit(solution)/shard_map/ppermute | solution.py:17
  24.2 1.1 copy-start.1
  24.2 1.1 copy-start.5
  25.7 7.6 %collective-permute-start.5 = (f32[2,1,64,256]{3,2,1,0:T(8,128)S(1)}, f32[2,1,64,256]{3,2,1,0:T(8,128)S(1)}, u32[]{:S(2)}, u32[]{:S(2)}) collective-permute-start(f32[2,1,64,256]{3,2,1,0:T(8,128)S(1)} %get-tuple-element.59), channel_id=1, source_target_pairs={{0,2},{2,4},{4,6},{6,8},{8,10},{10,12},{12,14},{1,3},{3,5},{5,7},{... | collective-permute-start | bytes 393224 | tf_op jit(solution)/shard_map/ppermute | solution.py:17
  30.1 7.4 %collective-permute-start.4 = (f32[2,1,64,256]{3,2,1,0:T(8,128)S(1)}, f32[2,1,64,256]{3,2,1,0:T(8,128)S(1)}, u32[]{:S(2)}, u32[]{:S(2)}) collective-permute-start(f32[2,1,64,256]{3,2,1,0:T(8,128)S(1)} %get-tuple-element.60), channel_id=1, source_target_pairs={{2,0},{4,2},{6,4},{8,6},{10,8},{12,10},{14,12},{3,1},{5,3},{7,5},{... | collective-permute-start | bytes 393224 | tf_op jit(solution)/shard_map/ppermute | solution.py:20
  37.5 4.3 %collective-permute-start.6 = (f32[2,6,1,256]{3,2,1,0:T(1,128)S(1)}, f32[2,6,1,256]{3,2,1,0:T(1,128)S(1)}, u32[]{:S(2)}, u32[]{:S(2)}) collective-permute-start(f32[2,6,1,256]{3,2,1,0:T(1,128)S(1)} %get-tuple-element.43), channel_id=1, source_target_pairs={{1,0},{3,2},{5,4},{7,6},{9,8},{11,10},{13,12},{15,14},{17,16},{19,... | collective-permute-start | bytes 36872 | tf_op jit(solution)/shard_map/ppermute | solution.py:20
  38.8 3.9 %collective-permute-start.7 = (f32[2,6,1,256]{3,2,1,0:T(1,128)S(1)}, f32[2,6,1,256]{3,2,1,0:T(1,128)S(1)}, u32[]{:S(2)}, u32[]{:S(2)}) collective-permute-start(f32[2,6,1,256]{3,2,1,0:T(1,128)S(1)} %get-tuple-element.44), channel_id=1, source_target_pairs={{0,1},{2,3},{4,5},{6,7},{8,9},{10,11},{12,13},{14,15},{16,17},{18,... | collective-permute-start | bytes 36872 | tf_op jit(solution)/shard_map/ppermute | solution.py:17
  43.3 7.8 %collective-permute-start.9 = (f32[2,1,64,256]{3,2,1,0:T(8,128)S(1)}, f32[2,1,64,256]{3,2,1,0:T(8,128)S(1)}, u32[]{:S(2)}, u32[]{:S(2)}) collective-permute-start(f32[2,1,64,256]{3,2,1,0:T(8,128)S(1)} %get-tuple-element.57), channel_id=1, source_target_pairs={{0,2},{2,4},{4,6},{6,8},{8,10},{10,12},{12,14},{1,3},{3,5},{5,7},{... | collective-permute-start | bytes 393224 | tf_op jit(solution)/shard_map/ppermute | solution.py:17
  47.8 7.4 %collective-permute-start.8 = (f32[2,1,64,256]{3,2,1,0:T(8,128)S(1)}, f32[2,1,64,256]{3,2,1,0:T(8,128)S(1)}, u32[]{:S(2)}, u32[]{:S(2)}) collective-permute-start(f32[2,1,64,256]{3,2,1,0:T(8,128)S(1)} %get-tuple-element.58), channel_id=1, source_target_pairs={{2,0},{4,2},{6,4},{8,6},{10,8},{12,10},{14,12},{3,1},{5,3},{7,5},{... | collective-permute-start | bytes 393224 | tf_op jit(solution)/shard_map/ppermute | solution.py:20
  55.2 4.3 %collective-permute-start.10 = (f32[2,6,1,256]{3,2,1,0:T(1,128)S(1)}, f32[2,6,1,256]{3,2,1,0:T(1,128)S(1)}, u32[]{:S(2)}, u32[]{:S(2)}) collective-permute-start(f32[2,6,1,256]{3,2,1,0:T(1,128)S(1)} %get-tuple-element.41), channel_id=1, source_target_pairs={{1,0},{3,2},{5,4},{7,6},{9,8},{11,10},{13,12},{15,14},{17,16},{19,... | collective-permute-start | bytes 36872 | tf_op jit(solution)/shard_map/ppermute | solution.py:20
  56.5 3.9 %collective-permute-start.11 = (f32[2,6,1,256]{3,2,1,0:T(1,128)S(1)}, f32[2,6,1,256]{3,2,1,0:T(1,128)S(1)}, u32[]{:S(2)}, u32[]{:S(2)}) collective-permute-start(f32[2,6,1,256]{3,2,1,0:T(1,128)S(1)} %get-tuple-element.42), channel_id=1, source_target_pairs={{0,1},{2,3},{4,5},{6,7},{8,9},{10,11},{12,13},{14,15},{16,17},{18,... | collective-permute-start | bytes 36872 | tf_op jit(solution)/shard_map/ppermute | solution.py:17
  61.0 7.2 %collective-permute-start.13 = (f32[2,1,64,256]{3,2,1,0:T(8,128)S(1)}, f32[2,1,64,256]{3,2,1,0:T(8,128)S(1)}, u32[]{:S(2)}, u32[]{:S(2)}) collective-permute-start(f32[2,1,64,256]{3,2,1,0:T(8,128)S(1)} %get-tuple-element.55), channel_id=1, source_target_pairs={{0,2},{2,4},{4,6},{6,8},{8,10},{10,12},{12,14},{1,3},{3,5},{5,7},{... | collective-permute-start | bytes 393224 | tf_op jit(solution)/shard_map/ppermute | solution.py:17
  65.0 7.4 %collective-permute-start.12 = (f32[2,1,64,256]{3,2,1,0:T(8,128)S(1)}, f32[2,1,64,256]{3,2,1,0:T(8,128)S(1)}, u32[]{:S(2)}, u32[]{:S(2)}) collective-permute-start(f32[2,1,64,256]{3,2,1,0:T(8,128)S(1)} %get-tuple-element.56), channel_id=1, source_target_pairs={{2,0},{4,2},{6,4},{8,6},{10,8},{12,10},{14,12},{3,1},{5,3},{7,5},{... | collective-permute-start | bytes 393224 | tf_op jit(solution)/shard_map/ppermute | solution.py:20
  72.4 4.3 %collective-permute-start.14 = (f32[2,6,1,256]{3,2,1,0:T(1,128)S(1)}, f32[2,6,1,256]{3,2,1,0:T(1,128)S(1)}, u32[]{:S(2)}, u32[]{:S(2)}) collective-permute-start(f32[2,6,1,256]{3,2,1,0:T(1,128)S(1)} %get-tuple-element.39), channel_id=1, source_target_pairs={{1,0},{3,2},{5,4},{7,6},{9,8},{11,10},{13,12},{15,14},{17,16},{19,... | collective-permute-start | bytes 36872 | tf_op jit(solution)/shard_map/ppermute | solution.py:20
  73.7 3.9 %collective-permute-start.15 = (f32[2,6,1,256]{3,2,1,0:T(1,128)S(1)}, f32[2,6,1,256]{3,2,1,0:T(1,128)S(1)}, u32[]{:S(2)}, u32[]{:S(2)}) collective-permute-start(f32[2,6,1,256]{3,2,1,0:T(1,128)S(1)} %get-tuple-element.40), channel_id=1, source_target_pairs={{0,1},{2,3},{4,5},{6,7},{8,9},{10,11},{12,13},{14,15},{16,17},{18,... | collective-permute-start | bytes 36872 | tf_op jit(solution)/shard_map/ppermute | solution.py:17
  78.2 7.2 %collective-permute-start.17 = (f32[2,1,64,256]{3,2,1,0:T(8,128)S(1)}, f32[2,1,64,256]{3,2,1,0:T(8,128)S(1)}, u32[]{:S(2)}, u32[]{:S(2)}) collective-permute-start(f32[2,1,64,256]{3,2,1,0:T(8,128)S(1)} %get-tuple-element.53), channel_id=1, source_target_pairs={{0,2},{2,4},{4,6},{6,8},{8,10},{10,12},{12,14},{1,3},{3,5},{5,7},{... | collective-permute-start | bytes 393224 | tf_op jit(solution)/shard_map/ppermute | solution.py:17
  82.2 13.5 %copy-start.8 = (f32[32,256]{1,0:T(8,128)S(1)}, f32[32,256]{1,0:T(8,128)}, u32[]{:S(2)}) copy-start(f32[32,256]{1,0:T(8,128)} %get-tuple-element.63) | copy-start | bytes 98308
  82.2 7.4 %collective-permute-start.16 = (f32[2,1,64,256]{3,2,1,0:T(8,128)S(1)}, f32[2,1,64,256]{3,2,1,0:T(8,128)S(1)}, u32[]{:S(2)}, u32[]{:S(2)}) collective-permute-start(f32[2,1,64,256]{3,2,1,0:T(8,128)S(1)} %get-tuple-element.54), channel_id=1, source_target_pairs={{2,0},{4,2},{6,4},{8,6},{10,8},{12,10},{14,12},{3,1},{5,3},{7,5},{... | collective-permute-start | bytes 393224 | tf_op jit(solution)/shard_map/ppermute | solution.py:20
  89.6 0.7 copy-start.6
  90.2 7.7 %collective-permute-start.18 = (f32[2,6,1,256]{3,2,1,0:T(1,128)}, f32[2,6,1,256]{3,2,1,0:T(1,128)}, u32[]{:S(2)}, u32[]{:S(2)}) collective-permute-start(f32[2,6,1,256]{3,2,1,0:T(1,128)} %get-tuple-element.37), channel_id=1, source_target_pairs={{1,0},{3,2},{5,4},{7,6},{9,8},{11,10},{13,12},{15,14},{17,16},{19,... | collective-permute-start | bytes 36872 | tf_op jit(solution)/shard_map/ppermute | solution.py:20
  91.5 6.4 %collective-permute-start.19 = (f32[2,6,1,256]{3,2,1,0:T(1,128)S(1)}, f32[2,6,1,256]{3,2,1,0:T(1,128)}, u32[]{:S(2)}, u32[]{:S(2)}) collective-permute-start(f32[2,6,1,256]{3,2,1,0:T(1,128)S(1)} %get-tuple-element.38), channel_id=1, source_target_pairs={{0,1},{2,3},{4,5},{6,7},{8,9},{10,11},{12,13},{14,15},{16,17},{18,... | collective-permute-start | bytes 36872 | tf_op jit(solution)/shard_map/ppermute | solution.py:17
  97.9 1.3 copy-start.3
  97.9 1.4 copy-start.7
  99.9 6.5 %collective-permute-start.21 = (f32[2,1,64,256]{3,2,1,0:T(8,128)S(1)}, f32[2,1,64,256]{3,2,1,0:T(8,128)S(1)}, u32[]{:S(2)}, u32[]{:S(2)}) collective-permute-start(f32[2,1,64,256]{3,2,1,0:T(8,128)S(1)} %get-tuple-element.51), channel_id=1, source_target_pairs={{0,2},{2,4},{4,6},{6,8},{8,10},{10,12},{12,14},{1,3},{3,5},{5,7},{... | collective-permute-start | bytes 393224 | tf_op jit(solution)/shard_map/ppermute | solution.py:17
  103.9 6.9 %collective-permute-start.20 = (f32[2,1,64,256]{3,2,1,0:T(8,128)S(1)}, f32[2,1,64,256]{3,2,1,0:T(8,128)S(1)}, u32[]{:S(2)}, u32[]{:S(2)}) collective-permute-start(f32[2,1,64,256]{3,2,1,0:T(8,128)S(1)} %get-tuple-element.52), channel_id=1, source_target_pairs={{2,0},{4,2},{6,4},{8,6},{10,8},{12,10},{14,12},{3,1},{5,3},{7,5},{... | collective-permute-start | bytes 393224 | tf_op jit(solution)/shard_map/ppermute | solution.py:20
  110.8 4.3 %collective-permute-start.22 = (f32[2,6,1,256]{3,2,1,0:T(1,128)S(1)}, f32[2,6,1,256]{3,2,1,0:T(1,128)S(1)}, u32[]{:S(2)}, u32[]{:S(2)}) collective-permute-start(f32[2,6,1,256]{3,2,1,0:T(1,128)S(1)} %get-tuple-element.35), channel_id=1, source_target_pairs={{1,0},{3,2},{5,4},{7,6},{9,8},{11,10},{13,12},{15,14},{17,16},{19,... | collective-permute-start | bytes 36872 | tf_op jit(solution)/shard_map/ppermute | solution.py:20
  112.1 3.9 %collective-permute-start.23 = (f32[2,6,1,256]{3,2,1,0:T(1,128)S(1)}, f32[2,6,1,256]{3,2,1,0:T(1,128)S(1)}, u32[]{:S(2)}, u32[]{:S(2)}) collective-permute-start(f32[2,6,1,256]{3,2,1,0:T(1,128)S(1)} %get-tuple-element.36), channel_id=1, source_target_pairs={{0,1},{2,3},{4,5},{6,7},{8,9},{10,11},{12,13},{14,15},{16,17},{18,... | collective-permute-start | bytes 36872 | tf_op jit(solution)/shard_map/ppermute | solution.py:17
  116.7 7.2 %collective-permute-start.25 = (f32[2,1,64,256]{3,2,1,0:T(8,128)S(1)}, f32[2,1,64,256]{3,2,1,0:T(8,128)S(1)}, u32[]{:S(2)}, u32[]{:S(2)}) collective-permute-start(f32[2,1,64,256]{3,2,1,0:T(8,128)S(1)} %get-tuple-element.49), channel_id=1, source_target_pairs={{0,2},{2,4},{4,6},{6,8},{8,10},{10,12},{12,14},{1,3},{3,5},{5,7},{... | collective-permute-start | bytes 393224 | tf_op jit(solution)/shard_map/ppermute | solution.py:17
  120.7 7.4 %collective-permute-start.24 = (f32[2,1,64,256]{3,2,1,0:T(8,128)S(1)}, f32[2,1,64,256]{3,2,1,0:T(8,128)S(1)}, u32[]{:S(2)}, u32[]{:S(2)}) collective-permute-start(f32[2,1,64,256]{3,2,1,0:T(8,128)S(1)} %get-tuple-element.50), channel_id=1, source_target_pairs={{2,0},{4,2},{6,4},{8,6},{10,8},{12,10},{14,12},{3,1},{5,3},{7,5},{... | collective-permute-start | bytes 393224 | tf_op jit(solution)/shard_map/ppermute | solution.py:20
  128.1 4.3 %collective-permute-start.26 = (f32[2,6,1,256]{3,2,1,0:T(1,128)S(1)}, f32[2,6,1,256]{3,2,1,0:T(1,128)S(1)}, u32[]{:S(2)}, u32[]{:S(2)}) collective-permute-start(f32[2,6,1,256]{3,2,1,0:T(1,128)S(1)} %get-tuple-element.33), channel_id=1, source_target_pairs={{1,0},{3,2},{5,4},{7,6},{9,8},{11,10},{13,12},{15,14},{17,16},{19,... | collective-permute-start | bytes 36872 | tf_op jit(solution)/shard_map/ppermute | solution.py:20
  129.4 3.9 %collective-permute-start.27 = (f32[2,6,1,256]{3,2,1,0:T(1,128)S(1)}, f32[2,6,1,256]{3,2,1,0:T(1,128)S(1)}, u32[]{:S(2)}, u32[]{:S(2)}) collective-permute-start(f32[2,6,1,256]{3,2,1,0:T(1,128)S(1)} %get-tuple-element.34), channel_id=1, source_target_pairs={{0,1},{2,3},{4,5},{6,7},{8,9},{10,11},{12,13},{14,15},{16,17},{18,... | collective-permute-start | bytes 36872 | tf_op jit(solution)/shard_map/ppermute | solution.py:17
  134.1 7.0 %collective-permute-start.29 = (f32[2,1,64,256]{3,2,1,0:T(8,128)S(1)}, f32[2,1,64,256]{3,2,1,0:T(8,128)S(1)}, u32[]{:S(2)}, u32[]{:S(2)}) collective-permute-start(f32[2,1,64,256]{3,2,1,0:T(8,128)S(1)} %get-tuple-element.47), channel_id=1, source_target_pairs={{0,2},{2,4},{4,6},{6,8},{8,10},{10,12},{12,14},{1,3},{3,5},{5,7},{... | collective-permute-start | bytes 393224 | tf_op jit(solution)/shard_map/ppermute | solution.py:17
  137.8 7.4 %collective-permute-start.28 = (f32[2,1,64,256]{3,2,1,0:T(8,128)S(1)}, f32[2,1,64,256]{3,2,1,0:T(8,128)S(1)}, u32[]{:S(2)}, u32[]{:S(2)}) collective-permute-start(f32[2,1,64,256]{3,2,1,0:T(8,128)S(1)} %get-tuple-element.48), channel_id=1, source_target_pairs={{2,0},{4,2},{6,4},{8,6},{10,8},{12,10},{14,12},{3,1},{5,3},{7,5},{... | collective-permute-start | bytes 393224 | tf_op jit(solution)/shard_map/ppermute | solution.py:20
  145.2 4.3 %collective-permute-start.30 = (f32[2,6,1,256]{3,2,1,0:T(1,128)S(1)}, f32[2,6,1,256]{3,2,1,0:T(1,128)S(1)}, u32[]{:S(2)}, u32[]{:S(2)}) collective-permute-start(f32[2,6,1,256]{3,2,1,0:T(1,128)S(1)} %get-tuple-element.31), channel_id=1, source_target_pairs={{1,0},{3,2},{5,4},{7,6},{9,8},{11,10},{13,12},{15,14},{17,16},{19,... | collective-permute-start | bytes 36872 | tf_op jit(solution)/shard_map/ppermute | solution.py:20
  146.5 3.9 %collective-permute-start.31 = (f32[2,6,1,256]{3,2,1,0:T(1,128)S(1)}, f32[2,6,1,256]{3,2,1,0:T(1,128)S(1)}, u32[]{:S(2)}, u32[]{:S(2)}) collective-permute-start(f32[2,6,1,256]{3,2,1,0:T(1,128)S(1)} %get-tuple-element.32), channel_id=1, source_target_pairs={{0,1},{2,3},{4,5},{6,7},{8,9},{10,11},{12,13},{14,15},{16,17},{18,... | collective-permute-start | bytes 36872 | tf_op jit(solution)/shard_map/ppermute | solution.py:17
  150.9 1.1 copy-start.2
  152.0 0.8 copy-start.4
Sparse Core Ops, SparseCore 0:
  153.8 68.6 all-reduce.9
where the time goes:
time: 233 us; the launch traced here: 232 us
  waiting for transfers between devices  86.4 us (37%)
  starting transfers between devices  80.2 us (34%)
  blocking collectives  32.2 us (14%)
  between operations  16.6 us (7%)
  other arithmetic  11 us (5%)
  local copies, waits for them, and re-layouts  5.59 us (2%)
    ppermute x16, starting transfers between devices, extended(): lax.ppermute(lax.slice_in_dim(block, block.shape[dim] - width, None, axis...  59.5 us
    psum x1, waiting for transfers between devices, on_device(): rows_sum = lax.psum(rows, 'gx')  35.9 us
    psum x1, blocking collectives, on_device(): squares = lax.psum(local_sq, ('gx', 'gy'))  32.2 us
    ppermute x16, waiting for transfers between devices, extended(): lax.ppermute(lax.slice_in_dim(block, 0, width, axis=dim), axis, backward)  29.1 us
    ppermute x16, waiting for transfers between devices, extended(): lax.ppermute(lax.slice_in_dim(block, block.shape[dim] - width, None, axis...  21.4 us
    ppermute x16, starting transfers between devices, extended(): lax.ppermute(lax.slice_in_dim(block, 0, width, axis=dim), axis, backward)  20.7 us
  transfers between devices with their start and end apart: 33, of which 23 were waited for; matrix products, arithmetic and copies ran while one was open for 2% of the time, Pallas kernels for 0%

commit v1 on v0

v1 whole, which is shorter than its diff:
```python
import functools
import math

import jax
import jax.numpy as jnp
from jax import lax
from jax.experimental import pallas as pl
from jax.experimental.pallas import tpu as pltpu
from jax.sharding import PartitionSpec as P

STEP_SIZE = 0.2
MESH = pl.DeviceIdType.MESH


def kernel(
    sections, planes, rows, chi, psi_late, psi_early, trap, controls,
    out, grad, power,
    field, psi, pot, coef, edge_in, edge_out, result, fine, ctl, prof, folded,
    late_rows, early_rows, far_power,
    x_send, x_recv, y_send, y_recv, t_send, t_recv, own_sem, o_send, o_recv,
    l_send, l_recv, e_send, e_recv, f_send, f_recv,
):
    deep, half, coarse = 2 * planes, rows // 2, rows // 4
    depth = chi.shape[3]
    pieces = depth // 128
    group = 2 * sections
    start = lax.axis_index("starts")
    g = lax.axis_index("gx")
    c = lax.axis_index("gy")
    x = lax.rem(g, 2)
    upper = lax.rem(x + c, 2)
    partner = g + 1 - 2 * x
    mine_at = pl.multiple_of(upper * half, half)
    other_at = pl.multiple_of((1 - upper) * half, half)
    mine_planes = x * planes
    other_planes = (1 - x) * planes
    has_low = g >= 2
    has_high = g < sections - 2

    def remote(src, dst, send, recv, to_g, to_c):
        return pltpu.make_async_remote_copy(
            src_ref=src, dst_ref=dst, send_sem=send, recv_sem=recv,
            device_id=(start, to_g, to_c), device_id_type=MESH,
        )

    mine = pl.ds(mine_at, half)
    own = [
        pltpu.make_async_copy(
            chi.at[:, :, mine, :], field.at[0, :, pl.ds(1 + mine_planes, planes)], own_sem.at[0]),
        pltpu.make_async_copy(
            psi_late.at[:, :, mine, :], psi.at[0, :, pl.ds(mine_planes, planes)], own_sem.at[1]),
        pltpu.make_async_copy(
            trap.at[:, mine, :], pot.at[pl.ds(mine_planes, planes)], own_sem.at[2]),
        pltpu.make_async_copy(
            psi_early.at[:, :, mine, :], psi.at[1, :, pl.ds(mine_planes, planes)], own_sem.at[3]),
        pltpu.make_async_copy(controls, ctl, own_sem.at[4]),
    ]
    for copy in own:
        copy.start()

    barrier = pltpu.get_barrier_semaphore()
    here = 2 * g + c

    def greet(d, _):
        there = lax.rem(here + d, group)
        pl.semaphore_signal(
            barrier, inc=1, device_id=(start, there // 2, lax.rem(there, 2)), device_id_type=MESH)
        return 0

    lax.fori_loop(1, group, greet, 0)
    pl.semaphore_wait(barrier, group - 1)

    theirs = pl.ds(other_at, half)

    def trade(src, dst, i):
        return remote(src, dst, t_send.at[i], t_recv.at[i], partner, c)

    def trades(at):
        part = pl.ds(at, planes)
        return [
            trade(chi.at[:, :, theirs, :], field.at[0, :, pl.ds(1 + at, planes)], 0),
            trade(psi_late.at[:, :, theirs, :], psi.at[0, :, part], 1),
            trade(trap.at[:, theirs, :], pot.at[part], 2),
        ] + [
            trade(psi_early.at[:, j, theirs, :], psi.at[1, :, at + j], 3 + j)
            for j in range(planes)
        ]

    sent = trades(mine_planes)
    arriving = trades(other_planes)
    for i in range(3):
        sent[i].start()

    stages = field.shape[0]
    blank = jnp.zeros((half, depth), jnp.float32)

    @pl.when(jnp.logical_not(has_low))
    def _():
        for s in range(stages):
            field[s, 0, 0] = blank
            field[s, 1, 0] = blank

    @pl.when(jnp.logical_not(has_high))
    def _():
        for s in range(stages):
            field[s, 0, deep + 1] = blank
            field[s, 1, deep + 1] = blank

    @pl.when(x == 0)
    def _():
        for s in range(stages):
            edge_in[s, upper] = jnp.zeros((2, deep, depth), jnp.float32)

    def low_copy(s):
        return remote(field.at[s, :, 1], field.at[s, :, deep + 1],
                      x_send.at[s, 0], x_recv.at[s, 1], g - 2, c)

    def high_copy(s):
        return remote(field.at[s, :, deep], field.at[s, :, 0],
                      x_send.at[s, 1], x_recv.at[s, 0], g + 2, c)

    def pair_copy(s):
        return remote(edge_out.at[s, 1 - upper], edge_in.at[s, upper],
                      y_send.at[s, 0], y_recv.at[s, 0], partner, c)

    def core_copy(s):
        return remote(edge_out.at[s, upper], edge_in.at[s, 1 - upper],
                      y_send.at[s, 1], y_recv.at[s, 1], g, 1 - c)

    def pair_arrival(s):
        return remote(edge_out.at[s, 1 - upper], edge_in.at[s, 1 - upper],
                      y_send.at[s, 0], y_recv.at[s, 0], partner, c)

    def core_arrival(s):
        return remote(edge_out.at[s, upper], edge_in.at[s, upper],
                      y_send.at[s, 1], y_recv.at[s, 1], g, 1 - c)

    def send_low(s):
        @pl.when(has_low)
        def _():
            low_copy(s).start()

    def send_high(s):
        @pl.when(has_high)
        def _():
            high_copy(s).start()

    def send_edges(s):
        pair_copy(s).start()

        @pl.when(x == 1)
        def _():
            core_copy(s).start()

    def wait_edges(s):
        pair_arrival(s).wait_recv()

        @pl.when(x == 1)
        def _():
            core_arrival(s).wait_recv()

    def wait_low(s):
        @pl.when(has_low)
        def _():
            high_copy(s).wait_recv()

    def wait_high(s):
        @pl.when(has_high)
        def _():
            low_copy(s).wait_recv()

    index = (g // 2) * deep + lax.broadcasted_iota(jnp.int32, (deep, depth), 0)
    prof[...] = 1.0 + 0.5 * jnp.cos(
        (2.0 * math.pi / (sections * planes)) * index.astype(jnp.float32))
    own[4].wait()
    for k in range(2):
        part = ctl[1 - k, pl.ds(pl.multiple_of(upper * coarse, coarse), coarse), :]
        for m in range(pieces):
            piece = part[:, m * 128:(m + 1) * 128]
            fine[k, m, pl.ds(0, coarse, stride=2), :] = piece
            fine[k, m, pl.ds(1, coarse, stride=2), :] = piece

    def coefficients(k, first):
        control = jnp.concatenate([fine[k, m] for m in range(pieces)], axis=1)

        def body(i, _):
            j = first + i
            p = psi[k, 0, j]
            q = psi[k, 1, j]
            base = pot[j] + prof[pl.ds(j, 1), :] * control + 3.0
            p2 = p * p
            q2 = q * q
            both = base + p2 + q2
            coef[k, 0, j] = STEP_SIZE * (both + 2.0 * p2)
            coef[k, 1, j] = (2.0 * STEP_SIZE) * (p * q)
            coef[k, 2, j] = STEP_SIZE * (both + 2.0 * q2)
            return 0

        lax.fori_loop(0, planes, body, 0)

    row = lax.broadcasted_iota(jnp.int32, (half, depth), 0)
    lane = lax.broadcasted_iota(jnp.int32, (half, depth), 1)
    first_row, last_row = row == 0, row == half - 1
    first_lane, last_lane = lane == 0, lane == depth - 1

    def neighbours(s, part, at, v):
        total = field[s, part, at - 1] + field[s, part, at + 1]
        total += jnp.where(
            first_row, edge_in[s, 0, part, pl.ds(at - 1, 1), :], pltpu.roll(v, 1, 0))
        total += jnp.where(
            last_row, edge_in[s, 1, part, pl.ds(at - 1, 1), :], pltpu.roll(v, half - 1, 0))
        total += jnp.where(first_lane, 0.0, pltpu.roll(v, 1, 1))
        total += jnp.where(last_lane, 0.0, pltpu.roll(v, depth - 1, 1))
        return total

    def term(s, at):
        k, n = s // 4, s % 4
        a = field[s, 0, at]
        b = field[s, 1, at]
        diag_a, mixed, diag_b = coef[k, 0, at - 1], coef[k, 1, at - 1], coef[k, 2, at - 1]
        up = diag_a * a + mixed * b - (0.5 * STEP_SIZE) * neighbours(s, 0, at, a)
        low = mixed * a + diag_b * b - (0.5 * STEP_SIZE) * neighbours(s, 1, at, b)
        a, b = low * (-1.0 / (n + 1)), up * (1.0 / (n + 1))
        if n == 3:
            for m in (3, 2, 1, 0):
                a += field[4 * k + m, 0, at]
                b += field[4 * k + m, 1, at]
        return a, b

    def put_edges(s, at, a, b):
        for part, v in ((0, a), (1, b)):
            edge_out[s, 0, part, pl.ds(at - 1, 1), :] = v[0:1]
            edge_out[s, 1, part, pl.ds(at - 1, 1), :] = v[half - 1:half]

    def overlap(k, at, a, b):
        weight = prof[pl.ds(at - 1, 1), :]
        return weight * (a * psi[k, 1, at - 1] - b * psi[k, 0, at - 1])

    def update(s, at, acc):
        a, b = term(s, at)
        field[s + 1, 0, at] = a
        field[s + 1, 1, at] = b
        put_edges(s + 1, at, a, b)
        if s == 3:
            acc = acc + overlap(0, at, a, b)
        return acc

    def fold(acc):
        for m in range(pieces):
            folded[m] = acc[:, m * 128:(m + 1) * 128]
        return jnp.concatenate(
            [folded[m, pl.ds(0, coarse, stride=2), :] + folded[m, pl.ds(1, coarse, stride=2), :]
             for m in range(pieces)], axis=1)

    own[0].wait()
    arriving[0].wait_recv()

    def first_edges(i, _):
        put_edges(0, i + 1, field[0, 0, i + 1], field[0, 1, i + 1])
        return 0

    send_low(0)
    send_high(0)
    lax.fori_loop(0, deep, first_edges, 0)
    send_edges(0)

    own[1].wait()
    own[2].wait()
    coefficients(0, mine_planes)
    arriving[1].wait_recv()
    arriving[2].wait_recv()
    sent[3].start()
    sent[4].start()
    coefficients(0, other_planes)

    late_sends = lambda d: remote(
        late_rows.at[g], late_rows.at[g], l_send.at[d], l_recv.at[g], lax.rem(g + d, sections), c)
    late_arrival = lambda d: remote(
        late_rows.at[g], late_rows.at[lax.rem(g + d, sections)], l_send.at[d],
        l_recv.at[lax.rem(g + d, sections)], lax.rem(g + d, sections), c)

    def loop(count, action):
        def body(d, _):
            action(d)
            return 0

        lax.fori_loop(1, count, body, 0)

    for s in range(stages - 1):
        acc = blank if s == 3 else 0
        wait_edges(s)
        if s == 3:
            acc = lax.fori_loop(2, deep, lambda at, t, s=s: update(s, at, t), acc)
        else:
            lax.fori_loop(2, deep, lambda at, t, s=s: update(s, at, t), 0)
        wait_low(s)
        acc = update(s, 1, acc)
        send_low(s + 1)
        wait_high(s)
        acc = update(s, deep, acc)
        send_high(s + 1)
        send_edges(s + 1)
        if s < planes - 2:
            sent[5 + s].start()
        if s == 3:
            late_rows[g] = fold(acc)
            loop(sections, lambda d: late_sends(d).start())
            own[3].wait()
            coefficients(1, mine_planes)
            for j in range(planes):
                arriving[3 + j].wait_recv()
            coefficients(1, other_planes)

    s = stages - 1

    def give(j):
        return remote(result.at[:, other_planes + j], out.at[:, j, mine, :],
                      o_send.at[j], o_recv.at[j], partner, c)

    def give_arrival(j):
        return remote(result.at[:, other_planes + j], out.at[:, j, theirs, :],
                      o_send.at[j], o_recv.at[j], partner, c)

    def finish(at, accs):
        acc, square = accs
        a, b = term(s, at)
        result[0, at - 1] = a
        result[1, at - 1] = b
        return acc + overlap(1, at, a, b), square + (a * a + b * b)

    accs = (blank, blank)
    wait_edges(s)
    inner_other = other_planes + x
    inner_mine = mine_planes + 1 - x

    def finish_send(i, accs):
        accs = finish(inner_other + i + 1, accs)
        give(x + i).start()
        return accs

    accs = lax.fori_loop(0, planes - 1, finish_send, accs)
    accs = lax.fori_loop(0, planes - 1, lambda i, t: finish(inner_mine + i + 1, t), accs)
    wait_low(s)
    wait_high(s)
    end_other = (1 - x) * (deep - 1)
    accs = finish(end_other + 1, accs)
    give((1 - x) * (planes - 1)).start()
    accs = finish(x * (deep - 1) + 1, accs)
    keep = pltpu.make_async_copy(
        result.at[:, pl.ds(mine_planes, planes)], out.at[:, :, mine, :], own_sem.at[0])
    keep.start()
    acc, square = accs
    early_rows[g, 0:coarse] = fold(acc)
    early_rows[g, coarse:coarse + 8] = jnp.sum(square.reshape(half // 8, 8, depth), axis=0)

    def early_copy(d, slot):
        return remote(early_rows.at[g], early_rows.at[slot], e_send.at[d], e_recv.at[slot],
                      lax.rem(g + d, sections), c)

    def far_copy(d, slot):
        return remote(early_rows.at[g, pl.ds(coarse, 8)], far_power.at[slot], f_send.at[d],
                      f_recv.at[slot], lax.rem(g + d, sections), 1 - c)

    far_copy(0, g).start()
    loop(sections, lambda d: (early_copy(d, g).start(), far_copy(d, g).start()))

    loop(sections, lambda d: late_arrival(d).wait_recv())

    def total(source, parity):
        value = source[parity, 0:coarse]
        return lax.fori_loop(
            1, sections // 2, lambda i, t: t + source[2 * i + parity, 0:coarse], value)

    late = [total(late_rows, c), total(late_rows, 1 - c)]
    far_copy(0, g).wait_recv()
    loop(sections, lambda d: (
        early_copy(d, lax.rem(g + d, sections)).wait_recv(),
        far_copy(d, lax.rem(g + d, sections)).wait_recv()))

    def squares(i, t):
        near, far = t
        return near + early_rows[i, coarse:coarse + 8], far + far_power[i]

    zero = jnp.zeros((8, depth), jnp.float32)
    near, far = lax.fori_loop(0, sections, squares, (zero, zero))
    mean = jnp.sum(near + far) / float(sections * planes * 2 * rows * depth)
    power[0] = mean
    scale = jnp.sqrt(float(sections * planes) * (jnp.full((coarse, depth), mean) + 1e-06))
    early = [total(early_rows, c), total(early_rows, 1 - c)]
    for i in range(2):
        grad[0, i * coarse:(i + 1) * coarse] = early[i] / scale
        grad[1, i * coarse:(i + 1) * coarse] = late[i] / scale

    for copy in sent:
        copy.wait_send()
    for s in range(stages):
        pair_copy(s).wait_send()

        @pl.when(x == 1)
        def _():
            core_copy(s).wait_send()

        @pl.when(has_low)
        def _():
            low_copy(s).wait_send()

        @pl.when(has_high)
        def _():
            high_copy(s).wait_send()

    loop(sections, lambda d: (late_sends(d).wait_send(), early_copy(d, g).wait_send(),
                              far_copy(d, g).wait_send()))
    far_copy(0, g).wait_send()
    keep.wait()
    for j in range(planes):
        give(j).wait_send()
        give_arrival(j).wait_recv()


def on_device(chi_final, psi_late, psi_early, trap, controls):
    planes, rows, depth = chi_final.shape[1:]
    sections = lax.axis_size("gx")
    deep, half, coarse = 2 * planes, rows // 2, rows // 4
    stages = 8
    f32 = jnp.float32
    anywhere = pl.BlockSpec(memory_space=pl.ANY)
    dma = pltpu.SemaphoreType.DMA
    return pl.pallas_call(
        functools.partial(kernel, sections, planes, rows),
        out_shape=(
            jax.ShapeDtypeStruct(chi_final.shape, f32),
            jax.ShapeDtypeStruct(controls.shape, f32),
            jax.ShapeDtypeStruct((1,), f32),
        ),
        in_specs=[anywhere] * 5,
        out_specs=(
            anywhere,
            pl.BlockSpec(memory_space=pltpu.VMEM),
            pl.BlockSpec(memory_space=pltpu.SMEM),
        ),
        scratch_shapes=[
            pltpu.VMEM((stages, 2, deep + 2, half, depth), f32),
            pltpu.VMEM((2, 2, deep, half, depth), f32),
            pltpu.VMEM((deep, half, depth), f32),
            pltpu.VMEM((2, 3, deep, half, depth), f32),
            pltpu.VMEM((stages, 2, 2, deep, depth), f32),
            pltpu.VMEM((stages, 2, 2, deep, depth), f32),
            pltpu.VMEM((2, deep, half, depth), f32),
            pltpu.VMEM((2, depth // 128, half, 128), f32),
            pltpu.VMEM(controls.shape, f32),
            pltpu.VMEM((deep, depth), f32),
            pltpu.VMEM((depth // 128, half, 128), f32),
            pltpu.VMEM((sections, coarse, depth), f32),
            pltpu.VMEM((sections, coarse + 8, depth), f32),
            pltpu.VMEM((sections, 8, depth), f32),
            dma((stages, 2)), dma((stages, 2)), dma((stages, 2)), dma((stages, 2)),
            dma((3 + planes,)), dma((3 + planes,)), dma((5,)), dma((planes,)), dma((planes,)),
            dma((sections,)), dma((sections,)), dma((sections,)), dma((sections,)),
            dma((sections,)), dma((sections,)),
        ],
        compiler_params=pltpu.CompilerParams(
            collective_id=0, has_side_effects=True, vmem_limit_bytes=32 * 1024 * 1024
        ),
        cost_estimate=pl.CostEstimate(
            flops=400 * planes * rows * depth, bytes_accessed=3_000_000, transcendentals=0),
    )(chi_final, psi_late, psi_early, trap, controls)


def solution(mesh):
    placed = (
        P(None, ("starts", "gx"), "gy", None),
        P(None, ("starts", "gx"), "gy", None),
        P(None, ("starts", "gx"), "gy", None),
        P("gx", "gy", None),
        P("starts", "gy", None),
    )
    return jax.shard_map(
        on_device,
        mesh=mesh,
        in_specs=placed,
        out_specs=(P(None, ("starts", "gx"), "gy", None), P("starts", "gy", None), P("starts")),
        check_vma=False,
    )
```

time: 233 us -> 71 us (0.30)
  waiting for transfers between devices: 86.4 us -> 0 us
  starting transfers between devices: 80.2 us -> 0 us
  Pallas kernels: 0 us -> 61.9 us
  blocking collectives: 32.2 us -> 0 us
  between operations: 16.6 us -> 2.34 us
  other arithmetic: 11 us -> 0 us
    ppermute x32 -> x0, starting transfers between devices: 80.2 us -> none  [the longest x16 59.5 us: extended(): lax.ppermute(lax.slice_in_dim(block, block.shape[dim] - width, None, axis...]
    pallas_call x0 -> x1, Pallas kernels: none -> 61.9 us  [on_device(): pl.pallas_call(functools.partial(kernel, sections, planes, rows), out_sha...]
    ppermute x32 -> x0, waiting for transfers between devices: 50.5 us -> none  [the longest x16 29.1 us: extended(): lax.ppermute(lax.slice_in_dim(block, 0, width, axis=dim), axis, backward)]
    psum x1 -> x0, waiting for transfers between devices: 35.9 us -> none  [on_device(): rows_sum = lax.psum(rows, 'gx')]
    psum x1 -> x0, blocking collectives: 32.2 us -> none  [on_device(): squares = lax.psum(local_sq, ('gx', 'gy'))]
    unnamed x20 -> x12, local copies, waits for them, and re-layouts: 0.68 us -> 6.33 us
    sub x8 -> x0, other arithmetic: 3.79 us -> none  [operator(): lapl = total - 6.0 * field]
  transfers between devices with their start and end apart: 33 -> 0, of which waited for: 23 -> 0; matrix products, arithmetic and copies ran while one was open for 2% -> 0% of each run, Pallas kernels for 0% -> 0%
where the time goes in v1:
time: 71 us; the launch traced here: 70.6 us
  Pallas kernels  61.9 us (87%)
  local copies, waits for them, and re-layouts  6.33 us (9%)
  between operations  2.34 us (3%)
    pallas_call x1, Pallas kernels, on_device(): pl.pallas_call(functools.partial(kernel, sections, planes, rows), out_sha...  61.9 us
    unnamed x12, local copies, waits for them, and re-layouts  6.33 us

profile of v1, /device:TPU:0, one launch (start us, length us, event | category | flops | bytes accessed | tf_op | source)
XLA Modules:
  0.0 70.6 jit_solution(1734378264674049136)
XLA Ops:
  0.6 0.0 copy-start
  0.6 1.0 %copy-done = f32[2,4,64,256]{3,2,1,0:T(8,128)S(1)} copy-done((f32[2,4,64,256]{3,2,1,0:T(8,128)S(1)}, f32[2,4,64,256]{3,2,1,0:T(8,128)}, u32[]{:S(2)}) %copy-start) | copy-done | bytes 524312
  1.7 0.0 copy-start.1
  1.7 1.0 %copy-done.1 = f32[2,4,64,256]{3,2,1,0:T(8,128)S(1)} copy-done((f32[2,4,64,256]{3,2,1,0:T(8,128)S(1)}, f32[2,4,64,256]{3,2,1,0:T(8,128)}, u32[]{:S(2)}) %copy-start.1) | copy-done | bytes 524312
  2.7 0.0 copy-start.2
  2.7 1.0 %copy-done.2 = f32[2,4,64,256]{3,2,1,0:T(8,128)S(1)} copy-done((f32[2,4,64,256]{3,2,1,0:T(8,128)S(1)}, f32[2,4,64,256]{3,2,1,0:T(8,128)}, u32[]{:S(2)}) %copy-start.2) | copy-done | bytes 524312
  3.8 0.0 copy-start.3
  3.8 0.9 %copy-done.3 = f32[4,64,256]{2,1,0:T(8,128)S(1)} copy-done((f32[4,64,256]{2,1,0:T(8,128)S(1)}, f32[4,64,256]{2,1,0:T(8,128)}, u32[]{:S(2)}) %copy-start.3) | copy-done | bytes 262168
  4.7 0.0 copy-start.4
  4.7 0.8 %copy-done.4 = f32[2,32,256]{2,1,0:T(8,128)S(1)} copy-done((f32[2,32,256]{2,1,0:T(8,128)S(1)}, f32[2,32,256]{2,1,0:T(8,128)}, u32[]{:S(2)}) %copy-start.4) | copy-done | bytes 65560
  5.5 61.9 %shard_map.76 = (f32[2,4,64,256]{3,2,1,0:T(8,128)S(1)}, f32[2,32,256]{2,1,0:T(8,128)S(1)}, f32[1]{0:T(128)}) custom-call(f32[2,4,64,256]{3,2,1,0:T(8,128)S(1)} %copy-done, f32[2,4,64,256]{3,2,1,0:T(8,128)S(1)} %copy-done.1, f32[2,4,64,256]{3,2,1,0:T(8,128)S(1)} %copy-done.2, f32[4,64,256]{2,1,0:T(8,128)S(1)} %copy-done.3, f32[2,32,256]{2,1,0:T(8,128)S(1)} %copy-done.4), custom_call_target="tpu_custom_call" | custom-call | flops 26214400 | bytes 3000000 | tf_op jit(solution)/shard_map/pallas_call | solution.py:428
  67.5 0.8 %copy.11 = f32[2,4,64,256]{3,2,1,0:T(8,128)} copy(f32[2,4,64,256]{3,2,1,0:T(8,128)S(1)} %get-tuple-element.6) | data formatting | bytes 1048576
  68.3 0.6 copy.12
Async XLA Ops:
  0.6 1.0 %copy-start = (f32[2,4,64,256]{3,2,1,0:T(8,128)S(1)}, f32[2,4,64,256]{3,2,1,0:T(8,128)}, u32[]{:S(2)}) copy-start(f32[2,4,64,256]{3,2,1,0:T(8,128)} %chi.1) | copy-start | bytes 1572868
  1.7 1.0 %copy-start.1 = (f32[2,4,64,256]{3,2,1,0:T(8,128)S(1)}, f32[2,4,64,256]{3,2,1,0:T(8,128)}, u32[]{:S(2)}) copy-start(f32[2,4,64,256]{3,2,1,0:T(8,128)} %psi_late.1) | copy-start | bytes 1572868
  2.7 1.0 %copy-start.2 = (f32[2,4,64,256]{3,2,1,0:T(8,128)S(1)}, f32[2,4,64,256]{3,2,1,0:T(8,128)}, u32[]{:S(2)}) copy-start(f32[2,4,64,256]{3,2,1,0:T(8,128)} %psi_early.1) | copy-start | bytes 1572868
  3.8 0.9 %copy-start.3 = (f32[4,64,256]{2,1,0:T(8,128)S(1)}, f32[4,64,256]{2,1,0:T(8,128)}, u32[]{:S(2)}) copy-start(f32[4,64,256]{2,1,0:T(8,128)} %trap.1) | copy-start | bytes 786436
  4.7 0.8 %copy-start.4 = (f32[2,32,256]{2,1,0:T(8,128)S(1)}, f32[2,32,256]{2,1,0:T(8,128)}, u32[]{:S(2)}) copy-start(f32[2,32,256]{2,1,0:T(8,128)} %controls.1) | copy-start | bytes 196612

commit v2 on v1

--- a/solution.py
+++ b/solution.py
@@ -15,7 +15,7 @@
 def kernel(
     sections, planes, rows, chi, psi_late, psi_early, trap, controls,
     out, grad, power,
-    field, psi, pot, coef, edge_in, edge_out, result, fine, ctl, prof, folded,
+    field, psi, pot, coef, edge_in, edge_out, rim_in, rim_out, result, fine, ctl, prof, folded,
     late_rows, early_rows, far_power,
     x_send, x_recv, y_send, y_recv, t_send, t_recv, own_sem, o_send, o_recv,
     l_send, l_recv, e_send, e_recv, f_send, f_recv,
@@ -75,21 +75,27 @@
     def trade(src, dst, i):
         return remote(src, dst, t_send.at[i], t_recv.at[i], partner, c)
 
-    def trades(at):
-        part = pl.ds(at, planes)
-        return [
-            trade(chi.at[:, :, theirs, :], field.at[0, :, pl.ds(1 + at, planes)], 0),
-            trade(psi_late.at[:, :, theirs, :], psi.at[0, :, part], 1),
-            trade(trap.at[:, theirs, :], pot.at[part], 2),
-        ] + [
-            trade(psi_early.at[:, j, theirs, :], psi.at[1, :, at + j], 3 + j)
-            for j in range(planes)
+    def trades(at, flag):
+        rim = flag * (planes - 1)
+        rest = pl.ds(1 - flag, planes - 1)
+        rest_to = pl.ds(at + 2 - flag, planes - 1)
+        moves = [
+            trade(chi.at[:, rim, theirs, :], field.at[0, :, 1 + at + rim], 0),
+            trade(chi.at[:, rest, theirs, :], field.at[0, :, rest_to], 1),
         ]
-
-    sent = trades(mine_planes)
-    arriving = trades(other_planes)
-    for i in range(3):
-        sent[i].start()
+        for j in range(planes):
+            moves.append(trade(psi_late.at[:, j, theirs, :], psi.at[0, :, at + j], 2 + 3 * j))
+            moves.append(trade(trap.at[j, theirs, :], pot.at[at + j], 3 + 3 * j))
+            moves.append(trade(psi_early.at[:, j, theirs, :], psi.at[1, :, at + j], 4 + 3 * j))
+        return moves
+
+    sent = trades(mine_planes, x)
+    arriving = trades(other_planes, 1 - x)
+    sent[0].start()
+    sent[1].start()
+    for j in range(planes):
+        sent[2 + 3 * j].start()
+        sent[3 + 3 * j].start()
 
     stages = field.shape[0]
     blank = jnp.zeros((half, depth), jnp.float32)
@@ -110,64 +116,75 @@
     def _():
         for s in range(stages):
             edge_in[s, upper] = jnp.zeros((2, deep, depth), jnp.float32)
-
-    def low_copy(s):
-        return remote(field.at[s, :, 1], field.at[s, :, deep + 1],
-                      x_send.at[s, 0], x_recv.at[s, 1], g - 2, c)
-
-    def high_copy(s):
-        return remote(field.at[s, :, deep], field.at[s, :, 0],
-                      x_send.at[s, 1], x_recv.at[s, 0], g + 2, c)
-
-    def pair_copy(s):
-        return remote(edge_out.at[s, 1 - upper], edge_in.at[s, upper],
-                      y_send.at[s, 0], y_recv.at[s, 0], partner, c)
-
-    def core_copy(s):
-        return remote(edge_out.at[s, upper], edge_in.at[s, 1 - upper],
-                      y_send.at[s, 1], y_recv.at[s, 1], g, 1 - c)
-
-    def pair_arrival(s):
-        return remote(edge_out.at[s, 1 - upper], edge_in.at[s, 1 - upper],
-                      y_send.at[s, 0], y_recv.at[s, 0], partner, c)
-
-    def core_arrival(s):
-        return remote(edge_out.at[s, upper], edge_in.at[s, upper],
-                      y_send.at[s, 1], y_recv.at[s, 1], g, 1 - c)
+            rim_in[s, upper] = jnp.zeros((8, depth), jnp.float32)
+
+    def low_copy(s, part):
+        return remote(field.at[s, part, 1], field.at[s, part, deep + 1],
+                      x_send.at[s, 0, part], x_recv.at[s, 1, part], g - 2, c)
+
+    def high_copy(s, part):
+        return remote(field.at[s, part, deep], field.at[s, part, 0],
+                      x_send.at[s, 1, part], x_recv.at[s, 0, part], g + 2, c)
+
+    boxes = ((edge_out, edge_in), (rim_out, rim_in))
+
+    def pair_copy(s, box):
+        source, target = boxes[box]
+        return remote(source.at[s, 1 - upper], target.at[s, upper],
+                      y_send.at[s, box, 0], y_recv.at[s, box, 0], partner, c)
+
+    def core_copy(s, box):
+        source, target = boxes[box]
+        return remote(source.at[s, upper], target.at[s, 1 - upper],
+                      y_send.at[s, box, 1], y_recv.at[s, box, 1], g, 1 - c)
+
+    def pair_arrival(s, box):
+        source, target = boxes[box]
+        return remote(source.at[s, 1 - upper], target.at[s, 1 - upper],
+                      y_send.at[s, box, 0], y_recv.at[s, box, 0], partner, c)
+
+    def core_arrival(s, box):
+        source, target = boxes[box]
+        return remote(source.at[s, upper], target.at[s, upper],
+                      y_send.at[s, box, 1], y_recv.at[s, box, 1], g, 1 - c)
 
     def send_low(s):
         @pl.when(has_low)
         def _():
-            low_copy(s).start()
+            low_copy(s, 0).start()
+            low_copy(s, 1).start()
 
     def send_high(s):
         @pl.when(has_high)
         def _():
-            high_copy(s).start()
-
-    def send_edges(s):
-        pair_copy(s).start()
+            high_copy(s, 0).start()
+            high_copy(s, 1).start()
+
+    def send_edges(s, box):
+        pair_copy(s, box).start()
 
         @pl.when(x == 1)
         def _():
-            core_copy(s).start()
-
-    def wait_edges(s):
-        pair_arrival(s).wait_recv()
+            core_copy(s, box).start()
+
+    def wait_edges(s, box):
+        pair_arrival(s, box).wait_recv()
 
         @pl.when(x == 1)
         def _():
-            core_arrival(s).wait_recv()
+            core_arrival(s, box).wait_recv()
 
     def wait_low(s):
         @pl.when(has_low)
         def _():
-            high_copy(s).wait_recv()
+            high_copy(s, 0).wait_recv()
+            high_copy(s, 1).wait_recv()
 
     def wait_high(s):
         @pl.when(has_high)
         def _():
-            low_copy(s).wait_recv()
+            low_copy(s, 0).wait_recv()
+            low_copy(s, 1).wait_recv()
 
     index = (g // 2) * deep + lax.broadcasted_iota(jnp.int32, (deep, depth), 0)
     prof[...] = 1.0 + 0.5 * jnp.cos(
@@ -180,7 +197,7 @@
             fine[k, m, pl.ds(0, coarse, stride=2), :] = piece
             fine[k, m, pl.ds(1, coarse, stride=2), :] = piece
 
-    def coefficients(k, first):
+    def coefficients(k, first, count):
         control = jnp.concatenate([fine[k, m] for m in range(pieces)], axis=1)
 
         def body(i, _):
@@ -196,30 +213,35 @@
             coef[k, 2, j] = STEP_SIZE * (both + 2.0 * q2)
             return 0
 
-        lax.fori_loop(0, planes, body, 0)
+        lax.fori_loop(0, count, body, 0)
 
     row = lax.broadcasted_iota(jnp.int32, (half, depth), 0)
     lane = lax.broadcasted_iota(jnp.int32, (half, depth), 1)
     first_row, last_row = row == 0, row == half - 1
     first_lane, last_lane = lane == 0, lane == depth - 1
 
-    def neighbours(s, part, at, v):
+    def edge_row(s, side, part, at, end):
+        if end is None:
+            return edge_in[s, side, part, pl.ds(at - 1, 1), :]
+        return rim_in[s, side, pl.ds(2 * part + end, 1), :]
+
+    def neighbours(s, part, at, v, end):
         total = field[s, part, at - 1] + field[s, part, at + 1]
         total += jnp.where(
-            first_row, edge_in[s, 0, part, pl.ds(at - 1, 1), :], pltpu.roll(v, 1, 0))
+            first_row, edge_row(s, 0, part, at, end), pltpu.roll(v, 1, 0))
         total += jnp.where(
-            last_row, edge_in[s, 1, part, pl.ds(at - 1, 1), :], pltpu.roll(v, half - 1, 0))
+            last_row, edge_row(s, 1, part, at, end), pltpu.roll(v, half - 1, 0))
         total += jnp.where(first_lane, 0.0, pltpu.roll(v, 1, 1))
         total += jnp.where(last_lane, 0.0, pltpu.roll(v, depth - 1, 1))
         return total
 
-    def term(s, at):
+    def term(s, at, end):
         k, n = s // 4, s % 4
         a = field[s, 0, at]
         b = field[s, 1, at]
         diag_a, mixed, diag_b = coef[k, 0, at - 1], coef[k, 1, at - 1], coef[k, 2, at - 1]
-        up = diag_a * a + mixed * b - (0.5 * STEP_SIZE) * neighbours(s, 0, at, a)
-        low = mixed * a + diag_b * b - (0.5 * STEP_SIZE) * neighbours(s, 1, at, b)
+        up = diag_a * a + mixed * b - (0.5 * STEP_SIZE) * neighbours(s, 0, at, a, end)
+        low = mixed * a + diag_b * b - (0.5 * STEP_SIZE) * neighbours(s, 1, at, b, end)
         a, b = low * (-1.0 / (n + 1)), up * (1.0 / (n + 1))
         if n == 3:
             for m in (3, 2, 1, 0):
@@ -227,20 +249,24 @@
                 b += field[4 * k + m, 1, at]
         return a, b
 
-    def put_edges(s, at, a, b):
+    def put_edges(s, at, a, b, end):
         for part, v in ((0, a), (1, b)):
-            edge_out[s, 0, part, pl.ds(at - 1, 1), :] = v[0:1]
-            edge_out[s, 1, part, pl.ds(at - 1, 1), :] = v[half - 1:half]
+            if end is None:
+                edge_out[s, 0, part, pl.ds(at - 1, 1), :] = v[0:1]
+                edge_out[s, 1, part, pl.ds(at - 1, 1), :] = v[half - 1:half]
+            else:
+                rim_out[s, 0, pl.ds(2 * part + end, 1), :] = v[0:1]
+                rim_out[s, 1, pl.ds(2 * part + end, 1), :] = v[half - 1:half]
 
     def overlap(k, at, a, b):
         weight = prof[pl.ds(at - 1, 1), :]
         return weight * (a * psi[k, 1, at - 1] - b * psi[k, 0, at - 1])
 
-    def update(s, at, acc):
-        a, b = term(s, at)
+    def update(s, at, acc, end=None):
+        a, b = term(s, at, end)
         field[s + 1, 0, at] = a
         field[s + 1, 1, at] = b
-        put_edges(s + 1, at, a, b)
+        put_edges(s + 1, at, a, b, end)
         if s == 3:
             acc = acc + overlap(0, at, a, b)
         return acc
@@ -253,25 +279,29 @@
              for m in range(pieces)], axis=1)
 
     own[0].wait()
+    own[1].wait()
+    own[2].wait()
+    coefficients(0, mine_planes, planes)
     arriving[0].wait_recv()
-
-    def first_edges(i, _):
-        put_edges(0, i + 1, field[0, 0, i + 1], field[0, 1, i + 1])
-        return 0
-
     send_low(0)
     send_high(0)
-    lax.fori_loop(0, deep, first_edges, 0)
-    send_edges(0)
-
-    own[1].wait()
-    own[2].wait()
-    coefficients(0, mine_planes)
+    put_edges(0, 1, field[0, 0, 1], field[0, 1, 1], 0)
+    put_edges(0, deep, field[0, 0, deep], field[0, 1, deep], 1)
+    send_edges(0, 1)
     arriving[1].wait_recv()
-    arriving[2].wait_recv()
-    sent[3].start()
+
+    def first_edges(at, _):
+        put_edges(0, at, field[0, 0, at], field[0, 1, at], None)
+        return 0
+
+    lax.fori_loop(2, deep, first_edges, 0)
+    send_edges(0, 0)
+    for j in range(planes):
+        arriving[2 + 3 * j].wait_recv()
+        arriving[3 + 3 * j].wait_recv()
+        coefficients(0, other_planes + j, 1)
     sent[4].start()
-    coefficients(0, other_planes)
+    sent[7].start()
 
     late_sends = lambda d: remote(
         late_rows.at[g], late_rows.at[g], l_send.at[d], l_recv.at[g], lax.rem(g + d, sections), c)
@@ -288,28 +318,32 @@
 
     for s in range(stages - 1):
         acc = blank if s == 3 else 0
-        wait_edges(s)
-        if s == 3:
-            acc = lax.fori_loop(2, deep, lambda at, t, s=s: update(s, at, t), acc)
-        else:
-            lax.fori_loop(2, deep, lambda at, t, s=s: update(s, at, t), 0)
+        wait_edges(s, 0)
+
+        def two(i, acc, s=s):
+            acc = update(s, 2 + 2 * i, acc)
+            return update(s, 3 + 2 * i, acc)
+
+        acc = lax.fori_loop(0, planes - 1, two, acc)
+        send_edges(s + 1, 0)
+        wait_edges(s, 1)
         wait_low(s)
-        acc = update(s, 1, acc)
+        acc = update(s, 1, acc, 0)
         send_low(s + 1)
         wait_high(s)
-        acc = update(s, deep, acc)
+        acc = update(s, deep, acc, 1)
         send_high(s + 1)
-        send_edges(s + 1)
+        send_edges(s + 1, 1)
         if s < planes - 2:
-            sent[5 + s].start()
+            sent[4 + 3 * (2 + s)].start()
         if s == 3:
             late_rows[g] = fold(acc)
             loop(sections, lambda d: late_sends(d).start())
             own[3].wait()
-            coefficients(1, mine_planes)
+            coefficients(1, mine_planes, planes)
             for j in range(planes):
-                arriving[3 + j].wait_recv()
-            coefficients(1, other_planes)
+                arriving[4 + 3 * j].wait_recv()
+            coefficients(1, other_planes, planes)
 
     s = stages - 1
 
@@ -321,15 +355,15 @@
         return remote(result.at[:, other_planes + j], out.at[:, j, theirs, :],
                       o_send.at[j], o_recv.at[j], partner, c)
 
-    def finish(at, accs):
+    def finish(at, accs, end=None):
         acc, square = accs
-        a, b = term(s, at)
+        a, b = term(s, at, end)
         result[0, at - 1] = a
         result[1, at - 1] = b
         return acc + overlap(1, at, a, b), square + (a * a + b * b)
 
     accs = (blank, blank)
-    wait_edges(s)
+    wait_edges(s, 0)
     inner_other = other_planes + x
     inner_mine = mine_planes + 1 - x
 
@@ -340,12 +374,12 @@
 
     accs = lax.fori_loop(0, planes - 1, finish_send, accs)
     accs = lax.fori_loop(0, planes - 1, lambda i, t: finish(inner_mine + i + 1, t), accs)
+    wait_edges(s, 1)
     wait_low(s)
     wait_high(s)
-    end_other = (1 - x) * (deep - 1)
-    accs = finish(end_other + 1, accs)
+    accs = finish((1 - x) * (deep - 1) + 1, accs, 1 - x)
     give((1 - x) * (planes - 1)).start()
-    accs = finish(x * (deep - 1) + 1, accs)
+    accs = finish(x * (deep - 1) + 1, accs, x)
     keep = pltpu.make_async_copy(
         result.at[:, pl.ds(mine_planes, planes)], out.at[:, :, mine, :], own_sem.at[0])
     keep.start()
@@ -394,19 +428,23 @@
     for copy in sent:
         copy.wait_send()
     for s in range(stages):
-        pair_copy(s).wait_send()
+        for box in range(2):
+            pair_copy(s, box).wait_send()
 
         @pl.when(x == 1)
         def _():
-            core_copy(s).wait_send()
+            for box in range(2):
+                core_copy(s, box).wait_send()
 
         @pl.when(has_low)
         def _():
-            low_copy(s).wait_send()
+            for part in range(2):
+                low_copy(s, part).wait_send()
 
         @pl.when(has_high)
         def _():
-            high_copy(s).wait_send()
+            for part in range(2):
+                high_copy(s, part).wait_send()
 
     loop(sections, lambda d: (late_sends(d).wait_send(), early_copy(d, g).wait_send(),
                               far_copy(d, g).wait_send()))
@@ -423,7 +461,7 @@
     deep, half, coarse = 2 * planes, rows // 2, rows // 4
     stages = 8
     f32 = jnp.float32
-    anywhere = pl.BlockSpec(memory_space=pl.ANY)
+    anywhere = pl.BlockSpec(memory_space=pltpu.HBM)
     dma = pltpu.SemaphoreType.DMA
     return pl.pallas_call(
         functools.partial(kernel, sections, planes, rows),
@@ -445,6 +483,8 @@
             pltpu.VMEM((2, 3, deep, half, depth), f32),
             pltpu.VMEM((stages, 2, 2, deep, depth), f32),
             pltpu.VMEM((stages, 2, 2, deep, depth), f32),
+            pltpu.VMEM((stages, 2, 8, depth), f32),
+            pltpu.VMEM((stages, 2, 8, depth), f32),
             pltpu.VMEM((2, deep, half, depth), f32),
             pltpu.VMEM((2, depth // 128, half, 128), f32),
             pltpu.VMEM(controls.shape, f32),
@@ -453,8 +493,8 @@
             pltpu.VMEM((sections, coarse, depth), f32),
             pltpu.VMEM((sections, coarse + 8, depth), f32),
             pltpu.VMEM((sections, 8, depth), f32),
-            dma((stages, 2)), dma((stages, 2)), dma((stages, 2)), dma((stages, 2)),
-            dma((3 + planes,)), dma((3 + planes,)), dma((5,)), dma((planes,)), dma((planes,)),
+            dma((stages, 2, 2)), dma((stages, 2, 2)), dma((stages, 2, 2)), dma((stages, 2, 2)),
+            dma((2 + 3 * planes,)), dma((2 + 3 * planes,)), dma((5,)), dma((planes,)), dma((planes,)),
             dma((sections,)), dma((sections,)), dma((sections,)), dma((sections,)),
             dma((sections,)), dma((sections,)),
         ],

time: 71 us -> 67.7 us (0.954)
  Pallas kernels: 61.9 us -> 58.7 us
    pallas_call x1, Pallas kernels: 61.9 us -> 58.7 us  [on_device(): pl.pallas_call(functools.partial(kernel, sections, planes, rows), out_sha...]
where the time goes in v2:
time: 67.7 us; the launch traced here: 67.4 us
  Pallas kernels  58.7 us (87%)
  local copies, waits for them, and re-layouts  6.33 us (9%)
  between operations  2.34 us (3%)
    pallas_call x1, Pallas kernels, on_device(): pl.pallas_call(functools.partial(kernel, sections, planes, rows), out_sha...  58.7 us
    unnamed x12, local copies, waits for them, and re-layouts  6.33 us

profile of v2, /device:TPU:0, one launch (start us, length us, event | category | flops | bytes accessed | tf_op | source)
XLA Modules:
  0.0 67.4 jit_solution(12716135616548588680)
XLA Ops:
  0.6 0.0 copy-start
  0.6 1.0 %copy-done = f32[2,4,64,256]{3,2,1,0:T(8,128)S(1)} copy-done((f32[2,4,64,256]{3,2,1,0:T(8,128)S(1)}, f32[2,4,64,256]{3,2,1,0:T(8,128)}, u32[]{:S(2)}) %copy-start) | copy-done | bytes 524312
  1.7 0.0 copy-start.1
  1.7 1.0 %copy-done.1 = f32[2,4,64,256]{3,2,1,0:T(8,128)S(1)} copy-done((f32[2,4,64,256]{3,2,1,0:T(8,128)S(1)}, f32[2,4,64,256]{3,2,1,0:T(8,128)}, u32[]{:S(2)}) %copy-start.1) | copy-done | bytes 524312
  2.7 0.0 copy-start.2
  2.7 1.0 %copy-done.2 = f32[2,4,64,256]{3,2,1,0:T(8,128)S(1)} copy-done((f32[2,4,64,256]{3,2,1,0:T(8,128)S(1)}, f32[2,4,64,256]{3,2,1,0:T(8,128)}, u32[]{:S(2)}) %copy-start.2) | copy-done | bytes 524312
  3.8 0.0 copy-start.3
  3.8 0.9 %copy-done.3 = f32[4,64,256]{2,1,0:T(8,128)S(1)} copy-done((f32[4,64,256]{2,1,0:T(8,128)S(1)}, f32[4,64,256]{2,1,0:T(8,128)}, u32[]{:S(2)}) %copy-start.3) | copy-done | bytes 262168
  4.7 0.0 copy-start.4
  4.7 0.8 %copy-done.4 = f32[2,32,256]{2,1,0:T(8,128)S(1)} copy-done((f32[2,32,256]{2,1,0:T(8,128)S(1)}, f32[2,32,256]{2,1,0:T(8,128)}, u32[]{:S(2)}) %copy-start.4) | copy-done | bytes 65560
  5.5 58.7 %shard_map.76 = (f32[2,4,64,256]{3,2,1,0:T(8,128)S(1)}, f32[2,32,256]{2,1,0:T(8,128)S(1)}, f32[1]{0:T(128)}) custom-call(f32[2,4,64,256]{3,2,1,0:T(8,128)S(1)} %copy-done, f32[2,4,64,256]{3,2,1,0:T(8,128)S(1)} %copy-done.1, f32[2,4,64,256]{3,2,1,0:T(8,128)S(1)} %copy-done.2, f32[4,64,256]{2,1,0:T(8,128)S(1)} %copy-done.3, f32[2,32,256]{2,1,0:T(8,128)S(1)} %copy-done.4), custom_call_target="tpu_custom_call" | custom-call | flops 26214400 | bytes 3000000 | tf_op jit(solution)/shard_map/pallas_call | solution.py:466
  64.2 0.8 %copy.11 = f32[2,4,64,256]{3,2,1,0:T(8,128)} copy(f32[2,4,64,256]{3,2,1,0:T(8,128)S(1)} %get-tuple-element.6) | data formatting | bytes 1048576
  65.0 0.6 copy.12
Async XLA Ops:
  0.6 1.0 %copy-start = (f32[2,4,64,256]{3,2,1,0:T(8,128)S(1)}, f32[2,4,64,256]{3,2,1,0:T(8,128)}, u32[]{:S(2)}) copy-start(f32[2,4,64,256]{3,2,1,0:T(8,128)} %chi.1) | copy-start | bytes 1572868
  1.7 1.0 %copy-start.1 = (f32[2,4,64,256]{3,2,1,0:T(8,128)S(1)}, f32[2,4,64,256]{3,2,1,0:T(8,128)}, u32[]{:S(2)}) copy-start(f32[2,4,64,256]{3,2,1,0:T(8,128)} %psi_late.1) | copy-start | bytes 1572868
  2.7 1.0 %copy-start.2 = (f32[2,4,64,256]{3,2,1,0:T(8,128)S(1)}, f32[2,4,64,256]{3,2,1,0:T(8,128)}, u32[]{:S(2)}) copy-start(f32[2,4,64,256]{3,2,1,0:T(8,128)} %psi_early.1) | copy-start | bytes 1572868
  3.8 0.9 %copy-start.3 = (f32[4,64,256]{2,1,0:T(8,128)S(1)}, f32[4,64,256]{2,1,0:T(8,128)}, u32[]{:S(2)}) copy-start(f32[4,64,256]{2,1,0:T(8,128)} %trap.1) | copy-start | bytes 786436
  4.7 0.8 %copy-start.4 = (f32[2,32,256]{2,1,0:T(8,128)S(1)}, f32[2,32,256]{2,1,0:T(8,128)}, u32[]{:S(2)}) copy-start(f32[2,32,256]{2,1,0:T(8,128)} %controls.1) | copy-start | bytes 196612

commit v3 on v2

--- a/solution.py
+++ b/solution.py
@@ -208,17 +208,17 @@
             p2 = p * p
             q2 = q * q
             both = base + p2 + q2
-            coef[k, 0, j] = STEP_SIZE * (both + 2.0 * p2)
-            coef[k, 1, j] = (2.0 * STEP_SIZE) * (p * q)
-            coef[k, 2, j] = STEP_SIZE * (both + 2.0 * q2)
+            coef[k, 0, j] = 2.0 * both + 4.0 * p2
+            coef[k, 1, j] = 4.0 * (p * q)
+            coef[k, 2, j] = 2.0 * both + 4.0 * q2
             return 0
 
         lax.fori_loop(0, count, body, 0)
 
-    row = lax.broadcasted_iota(jnp.int32, (half, depth), 0)
-    lane = lax.broadcasted_iota(jnp.int32, (half, depth), 1)
-    first_row, last_row = row == 0, row == half - 1
-    first_lane, last_lane = lane == 0, lane == depth - 1
+    row = lax.broadcasted_iota(jnp.int32, (8, depth), 0)
+    first_row, last_row = row == 0, row == 7
+    lane = lax.broadcasted_iota(jnp.int32, (half, 128), 1)
+    first_lane, last_lane = lane == 0, lane == 127
 
     def edge_row(s, side, part, at, end):
         if end is None:
@@ -227,22 +227,32 @@
 
     def neighbours(s, part, at, v, end):
         total = field[s, part, at - 1] + field[s, part, at + 1]
-        total += jnp.where(
-            first_row, edge_row(s, 0, part, at, end), pltpu.roll(v, 1, 0))
-        total += jnp.where(
-            last_row, edge_row(s, 1, part, at, end), pltpu.roll(v, half - 1, 0))
-        total += jnp.where(first_lane, 0.0, pltpu.roll(v, 1, 1))
-        total += jnp.where(last_lane, 0.0, pltpu.roll(v, depth - 1, 1))
-        return total
+        blocks = [v[i * 8:(i + 1) * 8] for i in range(half // 8)]
+        down = [edge_row(s, 0, part, at, end)] + [pltpu.roll(t, 1, 0) for t in blocks]
+        up = [pltpu.roll(t, 7, 0) for t in blocks] + [edge_row(s, 1, part, at, end)]
+        beside = [
+            jnp.where(first_row, down[i], down[i + 1]) + jnp.where(last_row, up[i + 1], up[i])
+            for i in range(half // 8)
+        ]
+        total = total + jnp.concatenate(beside, axis=0)
+        blocks = [v[:, i * 128:(i + 1) * 128] for i in range(pieces)]
+        down = [0.0] + [pltpu.roll(t, 1, 1) for t in blocks]
+        up = [pltpu.roll(t, 127, 1) for t in blocks] + [0.0]
+        beside = [
+            jnp.where(first_lane, down[i], down[i + 1]) + jnp.where(last_lane, up[i + 1], up[i])
+            for i in range(pieces)
+        ]
+        return total + jnp.concatenate(beside, axis=1)
 
     def term(s, at, end):
         k, n = s // 4, s % 4
         a = field[s, 0, at]
         b = field[s, 1, at]
         diag_a, mixed, diag_b = coef[k, 0, at - 1], coef[k, 1, at - 1], coef[k, 2, at - 1]
-        up = diag_a * a + mixed * b - (0.5 * STEP_SIZE) * neighbours(s, 0, at, a, end)
-        low = mixed * a + diag_b * b - (0.5 * STEP_SIZE) * neighbours(s, 1, at, b, end)
-        a, b = low * (-1.0 / (n + 1)), up * (1.0 / (n + 1))
+        up = diag_a * a + mixed * b - neighbours(s, 0, at, a, end)
+        low = mixed * a + diag_b * b - neighbours(s, 1, at, b, end)
+        scale = 0.5 * STEP_SIZE / (n + 1)
+        a, b = low * -scale, up * scale
         if n == 3:
             for m in (3, 2, 1, 0):
                 a += field[4 * k + m, 0, at]
@@ -499,7 +509,7 @@
             dma((sections,)), dma((sections,)),
         ],
         compiler_params=pltpu.CompilerParams(
-            collective_id=0, has_side_effects=True, vmem_limit_bytes=32 * 1024 * 1024
+            collective_id=0, has_side_effects=True, vmem_limit_bytes=63 * 1024 * 1024
         ),
         cost_estimate=pl.CostEstimate(
             flops=400 * planes * rows * depth, bytes_accessed=3_000_000, transcendentals=0),

time: 67.7 us -> 64.1 us (0.947)
  local copies, waits for them, and re-layouts: 6.33 us -> 2.53 us
    unnamed x12 -> x4, local copies, waits for them, and re-layouts: 6.33 us -> 2.53 us
where the time goes in v3:
time: 64.1 us; the launch traced here: 64 us
  Pallas kernels  59 us (92%)
  local copies, waits for them, and re-layouts  2.53 us (4%)
  between operations  2.46 us (4%)
    pallas_call x1, Pallas kernels, on_device(): pl.pallas_call(functools.partial(kernel, sections, planes, rows), out_sha...  59 us
    unnamed x4, local copies, waits for them, and re-layouts  2.53 us

profile of v3, /device:TPU:0, one launch (start us, length us, event | category | flops | bytes accessed | tf_op | source)
XLA Modules:
  0.0 64.0 jit_solution(5410043867252391507)
XLA Ops:
  0.6 59.0 %shard_map.76 = (f32[2,4,64,256]{3,2,1,0:T(8,128)}, f32[2,32,256]{2,1,0:T(8,128)}, f32[1]{0:T(128)}) custom-call(f32[2,4,64,256]{3,2,1,0:T(8,128)} %chi.1, f32[2,4,64,256]{3,2,1,0:T(8,128)} %psi_late.1, f32[2,4,64,256]{3,2,1,0:T(8,128)} %psi_early.1, f32[4,64,256]{2,1,0:T(8,128)} %trap.1, f32[2,32,256]{2,1,0:T(8,128)} %controls.1), custom_call_target="tpu_custom_call" | custom-call | flops 26214400 | bytes 3000000 | tf_op jit(solution)/shard_map/pallas_call | solution.py:476
  59.6 0.0 copy-start
  59.6 1.9 %copy.11 = f32[2,4,64,256]{3,2,1,0:T(8,128)} copy(f32[2,4,64,256]{3,2,1,0:T(8,128)} %get-tuple-element.6) | data formatting | bytes 1048576
  61.5 0.0 copy-done
  61.5 0.6 copy.12
Async XLA Ops:
  59.6 1.9 %copy-start = (f32[2,32,256]{2,1,0:T(8,128)S(1)}, f32[2,32,256]{2,1,0:T(8,128)}, u32[]{:S(2)}) copy-start(f32[2,32,256]{2,1,0:T(8,128)} %get-tuple-element.7) | copy-start | bytes 196612

commit v4 on v3

--- a/solution.py
+++ b/solution.py
@@ -76,26 +76,28 @@
         return remote(src, dst, t_send.at[i], t_recv.at[i], partner, c)
 
     def trades(at, flag):
-        rim = flag * (planes - 1)
-        rest = pl.ds(1 - flag, planes - 1)
-        rest_to = pl.ds(at + 2 - flag, planes - 1)
-        moves = [
-            trade(chi.at[:, rim, theirs, :], field.at[0, :, 1 + at + rim], 0),
-            trade(chi.at[:, rest, theirs, :], field.at[0, :, rest_to], 1),
-        ]
-        for j in range(planes):
-            moves.append(trade(psi_late.at[:, j, theirs, :], psi.at[0, :, at + j], 2 + 3 * j))
-            moves.append(trade(trap.at[j, theirs, :], pot.at[at + j], 3 + 3 * j))
-            moves.append(trade(psi_early.at[:, j, theirs, :], psi.at[1, :, at + j], 4 + 3 * j))
+        moves = []
+        for i in range(planes):
+            j = i + flag * (planes - 1 - 2 * i)
+            moves.append([
+                trade(chi.at[:, j, theirs, :], field.at[0, :, 1 + at + j], 4 * i),
+                trade(psi_late.at[:, j, theirs, :], psi.at[0, :, at + j], 4 * i + 1),
+                trade(trap.at[j, theirs, :], pot.at[at + j], 4 * i + 2),
+                trade(psi_early.at[:, j, theirs, :], psi.at[1, :, at + j], 4 * i + 3),
+            ])
         return moves
 
     sent = trades(mine_planes, x)
     arriving = trades(other_planes, 1 - x)
-    sent[0].start()
-    sent[1].start()
-    for j in range(planes):
-        sent[2 + 3 * j].start()
-        sent[3 + 3 * j].start()
+    sent[0][0].start()
+    sent[1][0].start()
+    sent[0][1].start()
+    sent[0][2].start()
+    for i in range(2, planes):
+        sent[i][0].start()
+    for i in range(1, planes):
+        sent[i][1].start()
+        sent[i][2].start()
 
     stages = field.shape[0]
     blank = jnp.zeros((half, depth), jnp.float32)
@@ -292,26 +294,20 @@
     own[1].wait()
     own[2].wait()
     coefficients(0, mine_planes, planes)
-    arriving[0].wait_recv()
+    arriving[0][0].wait_recv()
     send_low(0)
     send_high(0)
     put_edges(0, 1, field[0, 0, 1], field[0, 1, 1], 0)
     put_edges(0, deep, field[0, 0, deep], field[0, 1, deep], 1)
     send_edges(0, 1)
-    arriving[1].wait_recv()
+    arriving[1][0].wait_recv()
+    arriving[0][1].wait_recv()
+    arriving[0][2].wait_recv()
+    coefficients(0, (1 - x) * (deep - 1), 1)
 
     def first_edges(at, _):
         put_edges(0, at, field[0, 0, at], field[0, 1, at], None)
         return 0
-
-    lax.fori_loop(2, deep, first_edges, 0)
-    send_edges(0, 0)
-    for j in range(planes):
-        arriving[2 + 3 * j].wait_recv()
-        arriving[3 + 3 * j].wait_recv()
-        coefficients(0, other_planes + j, 1)
-    sent[4].start()
-    sent[7].start()
 
     late_sends = lambda d: remote(
         late_rows.at[g], late_rows.at[g], l_send.at[d], l_recv.at[g], lax.rem(g + d, sections), c)
@@ -328,14 +324,6 @@
 
     for s in range(stages - 1):
         acc = blank if s == 3 else 0
-        wait_edges(s, 0)
-
-        def two(i, acc, s=s):
-            acc = update(s, 2 + 2 * i, acc)
-            return update(s, 3 + 2 * i, acc)
-
-        acc = lax.fori_loop(0, planes - 1, two, acc)
-        send_edges(s + 1, 0)
         wait_edges(s, 1)
         wait_low(s)
         acc = update(s, 1, acc, 0)
@@ -344,15 +332,34 @@
         acc = update(s, deep, acc, 1)
         send_high(s + 1)
         send_edges(s + 1, 1)
-        if s < planes - 2:
-            sent[4 + 3 * (2 + s)].start()
+        if s == 0:
+            for i in range(2, planes):
+                arriving[i][0].wait_recv()
+            lax.fori_loop(2, deep, first_edges, 0)
+            send_edges(0, 0)
+            for i in range(1, planes):
+                arriving[i][1].wait_recv()
+                arriving[i][2].wait_recv()
+                coefficients(0, (1 - x) * (deep - 1) + i * (2 * x - 1), 1)
+            sent[0][3].start()
+            sent[1][3].start()
+        wait_edges(s, 0)
+
+        def two(i, acc, s=s):
+            acc = update(s, 2 + 2 * i, acc)
+            return update(s, 3 + 2 * i, acc)
+
+        acc = lax.fori_loop(0, planes - 1, two, acc)
+        send_edges(s + 1, 0)
+        if 1 <= s < planes - 1:
+            sent[s + 1][3].start()
         if s == 3:
             late_rows[g] = fold(acc)
             loop(sections, lambda d: late_sends(d).start())
             own[3].wait()
             coefficients(1, mine_planes, planes)
             for j in range(planes):
-                arriving[4 + 3 * j].wait_recv()
+                arriving[j][3].wait_recv()
             coefficients(1, other_planes, planes)
 
     s = stages - 1
@@ -435,8 +442,9 @@
         grad[0, i * coarse:(i + 1) * coarse] = early[i] / scale
         grad[1, i * coarse:(i + 1) * coarse] = late[i] / scale
 
-    for copy in sent:
-        copy.wait_send()
+    for moves in sent:
+        for copy in moves:
+            copy.wait_send()
     for s in range(stages):
         for box in range(2):
             pair_copy(s, box).wait_send()
@@ -463,6 +471,19 @@
     for j in range(planes):
         give(j).wait_send()
         give_arrival(j).wait_recv()
+
+
+def finish_kernel(field_in, grad_in, field_out, grad_out, sems):
+    planes = field_in.shape[1]
+    copies = [pltpu.make_async_copy(grad_in, grad_out, sems.at[2 * planes])]
+    for part in range(2):
+        for j in range(planes):
+            copies.append(pltpu.make_async_copy(
+                field_in.at[part, j], field_out.at[part, j], sems.at[part * planes + j]))
+    for copy in copies:
+        copy.start()
+    for copy in copies:
+        copy.wait()
 
 
 def on_device(chi_final, psi_late, psi_early, trap, controls):
@@ -473,7 +494,7 @@
     f32 = jnp.float32
     anywhere = pl.BlockSpec(memory_space=pltpu.HBM)
     dma = pltpu.SemaphoreType.DMA
-    return pl.pallas_call(
+    chi_start, grad_rows, power = pl.pallas_call(
         functools.partial(kernel, sections, planes, rows),
         out_shape=(
             jax.ShapeDtypeStruct(chi_final.shape, f32),
@@ -504,7 +525,7 @@
             pltpu.VMEM((sections, coarse + 8, depth), f32),
             pltpu.VMEM((sections, 8, depth), f32),
             dma((stages, 2, 2)), dma((stages, 2, 2)), dma((stages, 2, 2)), dma((stages, 2, 2)),
-            dma((2 + 3 * planes,)), dma((2 + 3 * planes,)), dma((5,)), dma((planes,)), dma((planes,)),
+            dma((4 * planes,)), dma((4 * planes,)), dma((5,)), dma((planes,)), dma((planes,)),
             dma((sections,)), dma((sections,)), dma((sections,)), dma((sections,)),
             dma((sections,)), dma((sections,)),
         ],
@@ -514,6 +535,18 @@
         cost_estimate=pl.CostEstimate(
             flops=400 * planes * rows * depth, bytes_accessed=3_000_000, transcendentals=0),
     )(chi_final, psi_late, psi_early, trap, controls)
+    chi_start, grad_rows = pl.pallas_call(
+        finish_kernel,
+        out_shape=(
+            jax.ShapeDtypeStruct(chi_final.shape, f32),
+            jax.ShapeDtypeStruct(controls.shape, f32),
+        ),
+        in_specs=[anywhere] * 2,
+        out_specs=(anywhere, anywhere),
+        scratch_shapes=[dma((2 * planes + 1,))],
+        compiler_params=pltpu.CompilerParams(vmem_limit_bytes=63 * 1024 * 1024),
+    )(chi_start, grad_rows)
+    return chi_start, grad_rows, power
 
 
 def solution(mesh):

time: 64.1 us -> 81.4 us (1.27)
  Pallas kernels: 59 us -> 78.8 us
  local copies, waits for them, and re-layouts: 2.53 us -> 0 us
    pallas_call x0 -> x1, Pallas kernels: none -> 19.1 us  [on_device(): pl.pallas_call(finish_kernel, out_shape=(jax.ShapeDtypeStruct(chi_final.s...]
    unnamed x4 -> x0, local copies, waits for them, and re-layouts: 2.53 us -> none
where the time goes in v4:
time: 81.4 us; the launch traced here: 81.3 us
  Pallas kernels  78.8 us (97%)
  between operations  2.45 us (3%)
    pallas_call x1, Pallas kernels, on_device(): pl.pallas_call(functools.partial(kernel, sections, planes, rows), out_sha...  59.8 us
    pallas_call x1, Pallas kernels, on_device(): pl.pallas_call(finish_kernel, out_shape=(jax.ShapeDtypeStruct(chi_final.s...  19.1 us

profile of v4, /device:TPU:0, one launch (start us, length us, event | category | flops | bytes accessed | tf_op | source)
XLA Modules:
  0.0 81.3 jit_solution(14663686499460551343)
XLA Ops:
  0.6 59.8 %shard_map.76 = (f32[2,4,64,256]{3,2,1,0:T(8,128)}, f32[2,32,256]{2,1,0:T(8,128)}, f32[1]{0:T(128)}) custom-call(f32[2,4,64,256]{3,2,1,0:T(8,128)} %chi.1, f32[2,4,64,256]{3,2,1,0:T(8,128)} %psi_late.1, f32[2,4,64,256]{3,2,1,0:T(8,128)} %psi_early.1, f32[4,64,256]{2,1,0:T(8,128)} %trap.1, f32[2,32,256]{2,1,0:T(8,128)} %controls.1), custom_call_target="tpu_custom_call" | custom-call | flops 26214400 | bytes 3000000 | tf_op jit(solution)/shard_map/pallas_call | solution.py:497
  60.4 19.1 %shard_map.77 = (f32[2,4,64,256]{3,2,1,0:T(8,128)}, f32[2,32,256]{2,1,0:T(8,128)}) custom-call(f32[2,4,64,256]{3,2,1,0:T(8,128)} %get-tuple-element.8.field_in, f32[2,32,256]{2,1,0:T(8,128)} %get-tuple-element.9.grad_in), custom_call_target="tpu_custom_call" | custom-call | tf_op jit(solution)/shard_map/pallas_call | solution.py:538

commit v5 on v4

--- a/solution.py
+++ b/solution.py
@@ -18,7 +18,7 @@
     field, psi, pot, coef, edge_in, edge_out, rim_in, rim_out, result, fine, ctl, prof, folded,
     late_rows, early_rows, far_power,
     x_send, x_recv, y_send, y_recv, t_send, t_recv, own_sem, o_send, o_recv,
-    l_send, l_recv, e_send, e_recv, f_send, f_recv,
+    l_send, l_recv, e_send, e_recv, f_send, f_recv, give_chi, give_psi, give_trap, back,
 ):
     deep, half, coarse = 2 * planes, rows // 2, rows // 4
     depth = chi.shape[3]
@@ -55,6 +55,15 @@
             psi_early.at[:, :, mine, :], psi.at[1, :, pl.ds(mine_planes, planes)], own_sem.at[3]),
         pltpu.make_async_copy(controls, ctl, own_sem.at[4]),
     ]
+    theirs = pl.ds(other_at, half)
+    staged = [
+        pltpu.make_async_copy(chi.at[:, :, theirs, :], give_chi, own_sem.at[5]),
+        pltpu.make_async_copy(psi_late.at[:, :, theirs, :], give_psi.at[0], own_sem.at[6]),
+        pltpu.make_async_copy(trap.at[:, theirs, :], give_trap, own_sem.at[7]),
+        pltpu.make_async_copy(psi_early.at[:, :, theirs, :], give_psi.at[1], own_sem.at[8]),
+    ]
+    for copy in staged:
+        copy.start()
     for copy in own:
         copy.start()
 
@@ -70,7 +79,8 @@
     lax.fori_loop(1, group, greet, 0)
     pl.semaphore_wait(barrier, group - 1)
 
-    theirs = pl.ds(other_at, half)
+    for copy in staged:
+        copy.wait()
 
     def trade(src, dst, i):
         return remote(src, dst, t_send.at[i], t_recv.at[i], partner, c)
@@ -80,10 +90,10 @@
         for i in range(planes):
             j = i + flag * (planes - 1 - 2 * i)
             moves.append([
-                trade(chi.at[:, j, theirs, :], field.at[0, :, 1 + at + j], 4 * i),
-                trade(psi_late.at[:, j, theirs, :], psi.at[0, :, at + j], 4 * i + 1),
-                trade(trap.at[j, theirs, :], pot.at[at + j], 4 * i + 2),
-                trade(psi_early.at[:, j, theirs, :], psi.at[1, :, at + j], 4 * i + 3),
+                trade(give_chi.at[:, j], field.at[0, :, 1 + at + j], 4 * i),
+                trade(give_psi.at[0, :, j], psi.at[0, :, at + j], 4 * i + 1),
+                trade(give_trap.at[j], pot.at[at + j], 4 * i + 2),
+                trade(give_psi.at[1, :, j], psi.at[1, :, at + j], 4 * i + 3),
             ])
         return moves
 
@@ -120,13 +130,13 @@
             edge_in[s, upper] = jnp.zeros((2, deep, depth), jnp.float32)
             rim_in[s, upper] = jnp.zeros((8, depth), jnp.float32)
 
-    def low_copy(s, part):
-        return remote(field.at[s, part, 1], field.at[s, part, deep + 1],
-                      x_send.at[s, 0, part], x_recv.at[s, 1, part], g - 2, c)
-
-    def high_copy(s, part):
-        return remote(field.at[s, part, deep], field.at[s, part, 0],
-                      x_send.at[s, 1, part], x_recv.at[s, 0, part], g + 2, c)
+    def low_copy(s):
+        return remote(field.at[s, :, 1], field.at[s, :, deep + 1],
+                      x_send.at[s, 0], x_recv.at[s, 1], g - 2, c)
+
+    def high_copy(s):
+        return remote(field.at[s, :, deep], field.at[s, :, 0],
+                      x_send.at[s, 1], x_recv.at[s, 0], g + 2, c)
 
     boxes = ((edge_out, edge_in), (rim_out, rim_in))
 
@@ -153,14 +163,12 @@
     def send_low(s):
         @pl.when(has_low)
         def _():
-            low_copy(s, 0).start()
-            low_copy(s, 1).start()
+            low_copy(s).start()
 
     def send_high(s):
         @pl.when(has_high)
         def _():
-            high_copy(s, 0).start()
-            high_copy(s, 1).start()
+            high_copy(s).start()
 
     def send_edges(s, box):
         pair_copy(s, box).start()
@@ -179,14 +187,29 @@
     def wait_low(s):
         @pl.when(has_low)
         def _():
-            high_copy(s, 0).wait_recv()
-            high_copy(s, 1).wait_recv()
+            high_copy(s).wait_recv()
 
     def wait_high(s):
         @pl.when(has_high)
         def _():
-            low_copy(s, 0).wait_recv()
-            low_copy(s, 1).wait_recv()
+            low_copy(s).wait_recv()
+
+    def settle(s):
+        for box in range(2):
+            pair_copy(s, box).wait_send()
+
+        @pl.when(x == 1)
+        def _():
+            for box in range(2):
+                core_copy(s, box).wait_send()
+
+        @pl.when(has_low)
+        def _():
+            low_copy(s).wait_send()
+
+        @pl.when(has_high)
+        def _():
+            high_copy(s).wait_send()
 
     index = (g // 2) * deep + lax.broadcasted_iota(jnp.int32, (deep, depth), 0)
     prof[...] = 1.0 + 0.5 * jnp.cos(
@@ -322,6 +345,11 @@
 
         lax.fori_loop(1, count, body, 0)
 
+    def total(source, parity):
+        value = source[parity, 0:coarse]
+        return lax.fori_loop(
+            1, sections // 2, lambda i, t: t + source[2 * i + parity, 0:coarse], value)
+
     for s in range(stages - 1):
         acc = blank if s == 3 else 0
         wait_edges(s, 1)
@@ -332,6 +360,8 @@
         acc = update(s, deep, acc, 1)
         send_high(s + 1)
         send_edges(s + 1, 1)
+        if 1 <= s < planes:
+            sent[s][3].start()
         if s == 0:
             for i in range(2, planes):
                 arriving[i][0].wait_recv()
@@ -342,7 +372,6 @@
                 arriving[i][2].wait_recv()
                 coefficients(0, (1 - x) * (deep - 1) + i * (2 * x - 1), 1)
             sent[0][3].start()
-            sent[1][3].start()
         wait_edges(s, 0)
 
         def two(i, acc, s=s):
@@ -351,8 +380,16 @@
 
         acc = lax.fori_loop(0, planes - 1, two, acc)
         send_edges(s + 1, 0)
-        if 1 <= s < planes - 1:
-            sent[s + 1][3].start()
+        settle(s)
+        if s == 4:
+            for moves in sent:
+                for copy in moves:
+                    copy.wait_send()
+        if s == 6:
+            loop(sections, lambda d: late_arrival(d).wait_recv())
+            loop(sections, lambda d: late_sends(d).wait_send())
+            for i, parity in enumerate((c, 1 - c)):
+                grad[1, i * coarse:(i + 1) * coarse] = total(late_rows, parity)
         if s == 3:
             late_rows[g] = fold(acc)
             loop(sections, lambda d: late_sends(d).start())
@@ -365,12 +402,11 @@
     s = stages - 1
 
     def give(j):
-        return remote(result.at[:, other_planes + j], out.at[:, j, mine, :],
+        return remote(result.at[:, other_planes + j], back.at[:, j],
                       o_send.at[j], o_recv.at[j], partner, c)
 
-    def give_arrival(j):
-        return remote(result.at[:, other_planes + j], out.at[:, j, theirs, :],
-                      o_send.at[j], o_recv.at[j], partner, c)
+    def put_back(j):
+        return pltpu.make_async_copy(back.at[:, j], out.at[:, j, theirs, :], own_sem.at[9 + j])
 
     def finish(at, accs, end=None):
         acc, square = accs
@@ -415,14 +451,12 @@
     far_copy(0, g).start()
     loop(sections, lambda d: (early_copy(d, g).start(), far_copy(d, g).start()))
 
-    loop(sections, lambda d: late_arrival(d).wait_recv())
-
-    def total(source, parity):
-        value = source[parity, 0:coarse]
-        return lax.fori_loop(
-            1, sections // 2, lambda i, t: t + source[2 * i + parity, 0:coarse], value)
-
-    late = [total(late_rows, c), total(late_rows, 1 - c)]
+    settle(s)
+    for j in range(planes):
+        give(j).wait_send()
+    for j in range(planes):
+        give(j).wait_recv()
+        put_back(j).start()
     far_copy(0, g).wait_recv()
     loop(sections, lambda d: (
         early_copy(d, lax.rem(g + d, sections)).wait_recv(),
@@ -440,49 +474,29 @@
     early = [total(early_rows, c), total(early_rows, 1 - c)]
     for i in range(2):
         grad[0, i * coarse:(i + 1) * coarse] = early[i] / scale
-        grad[1, i * coarse:(i + 1) * coarse] = late[i] / scale
-
-    for moves in sent:
-        for copy in moves:
-            copy.wait_send()
-    for s in range(stages):
-        for box in range(2):
-            pair_copy(s, box).wait_send()
-
-        @pl.when(x == 1)
-        def _():
-            for box in range(2):
-                core_copy(s, box).wait_send()
-
-        @pl.when(has_low)
-        def _():
-            for part in range(2):
-                low_copy(s, part).wait_send()
-
-        @pl.when(has_high)
-        def _():
-            for part in range(2):
-                high_copy(s, part).wait_send()
-
-    loop(sections, lambda d: (late_sends(d).wait_send(), early_copy(d, g).wait_send(),
-                              far_copy(d, g).wait_send()))
+        grad[1, i * coarse:(i + 1) * coarse] = grad[1, i * coarse:(i + 1) * coarse] / scale
+
+    loop(sections, lambda d: (early_copy(d, g).wait_send(), far_copy(d, g).wait_send()))
     far_copy(0, g).wait_send()
     keep.wait()
     for j in range(planes):
-        give(j).wait_send()
-        give_arrival(j).wait_recv()
-
-
-def finish_kernel(field_in, grad_in, field_out, grad_out, sems):
+        put_back(j).wait()
+
+
+def finish_kernel(field_in, grad_in, field_out, grad_out, held, held_grad, sems):
     planes = field_in.shape[1]
-    copies = [pltpu.make_async_copy(grad_in, grad_out, sems.at[2 * planes])]
+    moves = [(grad_in, held_grad, grad_out)]
     for part in range(2):
         for j in range(planes):
-            copies.append(pltpu.make_async_copy(
-                field_in.at[part, j], field_out.at[part, j], sems.at[part * planes + j]))
-    for copy in copies:
+            moves.append((field_in.at[part, j], held.at[part, j], field_out.at[part, j]))
+    arrive = [pltpu.make_async_copy(a, b, sems.at[0, i]) for i, (a, b, _) in enumerate(moves)]
+    leave = [pltpu.make_async_copy(b, o, sems.at[1, i]) for i, (_, b, o) in enumerate(moves)]
+    for copy in arrive:
         copy.start()
-    for copy in copies:
+    for copy, then in zip(arrive, leave):
+        copy.wait()
+        then.start()
+    for copy in leave:
         copy.wait()
 
 
@@ -524,10 +538,14 @@
             pltpu.VMEM((sections, coarse, depth), f32),
             pltpu.VMEM((sections, coarse + 8, depth), f32),
             pltpu.VMEM((sections, 8, depth), f32),
-            dma((stages, 2, 2)), dma((stages, 2, 2)), dma((stages, 2, 2)), dma((stages, 2, 2)),
-            dma((4 * planes,)), dma((4 * planes,)), dma((5,)), dma((planes,)), dma((planes,)),
+            dma((stages, 2)), dma((stages, 2)), dma((stages, 2, 2)), dma((stages, 2, 2)),
+            dma((4 * planes,)), dma((4 * planes,)), dma((9 + planes,)), dma((planes,)), dma((planes,)),
             dma((sections,)), dma((sections,)), dma((sections,)), dma((sections,)),
             dma((sections,)), dma((sections,)),
+            pltpu.VMEM((2, planes, half, depth), f32),
+            pltpu.VMEM((2, 2, planes, half, depth), f32),
+            pltpu.VMEM((planes, half, depth), f32),
+            pltpu.VMEM((2, planes, half, depth), f32),
         ],
         compiler_params=pltpu.CompilerParams(
             collective_id=0, has_side_effects=True, vmem_limit_bytes=63 * 1024 * 1024
@@ -543,7 +561,11 @@
         ),
         in_specs=[anywhere] * 2,
         out_specs=(anywhere, anywhere),
-        scratch_shapes=[dma((2 * planes + 1,))],
+        scratch_shapes=[
+            pltpu.VMEM(chi_final.shape, f32),
+            pltpu.VMEM(controls.shape, f32),
+            dma((2, 2 * planes + 1)),
+        ],
         compiler_params=pltpu.CompilerParams(vmem_limit_bytes=63 * 1024 * 1024),
     )(chi_start, grad_rows)
     return chi_start, grad_rows, power

time: 81.4 us -> 63.8 us (0.78)
  Pallas kernels: 78.8 us -> 61.2 us
    pallas_call x1, Pallas kernels: 19.1 us -> 1.88 us  [on_device(): pl.pallas_call(finish_kernel, out_shape=(jax.ShapeDtypeStruct(chi_final.s...]
where the time goes in v5:
time: 63.8 us; the launch traced here: 63.6 us
  Pallas kernels  61.2 us (96%)
  between operations  2.45 us (4%)
    pallas_call x1, Pallas kernels, on_device(): pl.pallas_call(functools.partial(kernel, sections, planes, rows), out_sha...  59.3 us
    pallas_call x1, Pallas kernels, on_device(): pl.pallas_call(finish_kernel, out_shape=(jax.ShapeDtypeStruct(chi_final.s...  1.88 us

profile of v5, /device:TPU:0, one launch (start us, length us, event | category | flops | bytes accessed | tf_op | source)
XLA Modules:
  0.0 63.6 jit_solution(4687657600246544790)
XLA Ops:
  0.6 59.3 %shard_map.76 = (f32[2,4,64,256]{3,2,1,0:T(8,128)}, f32[2,32,256]{2,1,0:T(8,128)}, f32[1]{0:T(128)}) custom-call(f32[2,4,64,256]{3,2,1,0:T(8,128)} %chi.1, f32[2,4,64,256]{3,2,1,0:T(8,128)} %psi_late.1, f32[2,4,64,256]{3,2,1,0:T(8,128)} %psi_early.1, f32[4,64,256]{2,1,0:T(8,128)} %trap.1, f32[2,32,256]{2,1,0:T(8,128)} %controls.1), custom_call_target="tpu_custom_call" | custom-call | flops 26214400 | bytes 3000000 | tf_op jit(solution)/shard_map/pallas_call | solution.py:511
  59.9 1.9 %shard_map.77 = (f32[2,4,64,256]{3,2,1,0:T(8,128)}, f32[2,32,256]{2,1,0:T(8,128)}) custom-call(f32[2,4,64,256]{3,2,1,0:T(8,128)} %get-tuple-element.8.field_in, f32[2,32,256]{2,1,0:T(8,128)} %get-tuple-element.9.grad_in), custom_call_target="tpu_custom_call" | custom-call | tf_op jit(solution)/shard_map/pallas_call | solution.py:556

commit v6 on v5

--- a/solution.py
+++ b/solution.py
@@ -99,15 +99,20 @@
 
     sent = trades(mine_planes, x)
     arriving = trades(other_planes, 1 - x)
-    sent[0][0].start()
-    sent[1][0].start()
-    sent[0][1].start()
-    sent[0][2].start()
-    for i in range(2, planes):
-        sent[i][0].start()
+    queue = [sent[0][0], sent[1][0], sent[0][1], sent[0][2]]
+    queue += [sent[i][0] for i in range(2, planes)]
     for i in range(1, planes):
-        sent[i][1].start()
-        sent[i][2].start()
+        queue += [sent[i][1], sent[i][2]]
+    queue += [sent[i][3] for i in range(planes)]
+    bulk = len(queue) - planes
+    flying = 3
+    for copy in queue[:flying]:
+        copy.start()
+
+    def advance(first, last):
+        for i in range(first, last):
+            queue[i - flying].wait_send()
+            queue[i].start()
 
     stages = field.shape[0]
     blank = jnp.zeros((half, depth), jnp.float32)
@@ -317,12 +322,14 @@
     own[1].wait()
     own[2].wait()
     coefficients(0, mine_planes, planes)
+    advance(flying, 5)
     arriving[0][0].wait_recv()
     send_low(0)
     send_high(0)
     put_edges(0, 1, field[0, 0, 1], field[0, 1, 1], 0)
     put_edges(0, deep, field[0, 0, deep], field[0, 1, deep], 1)
     send_edges(0, 1)
+    advance(5, 7)
     arriving[1][0].wait_recv()
     arriving[0][1].wait_recv()
     arriving[0][2].wait_recv()
@@ -351,6 +358,8 @@
             1, sections // 2, lambda i, t: t + source[2 * i + parity, 0:coarse], value)
 
     for s in range(stages - 1):
+        if s == 0:
+            advance(7, 8)
         acc = blank if s == 3 else 0
         wait_edges(s, 1)
         wait_low(s)
@@ -361,17 +370,18 @@
         send_high(s + 1)
         send_edges(s + 1, 1)
         if 1 <= s < planes:
-            sent[s][3].start()
+            advance(bulk + s, bulk + s + 1)
         if s == 0:
             for i in range(2, planes):
                 arriving[i][0].wait_recv()
             lax.fori_loop(2, deep, first_edges, 0)
             send_edges(0, 0)
             for i in range(1, planes):
+                advance(min(planes + 2 + 2 * i, bulk), min(planes + 4 + 2 * i, bulk))
                 arriving[i][1].wait_recv()
                 arriving[i][2].wait_recv()
                 coefficients(0, (1 - x) * (deep - 1) + i * (2 * x - 1), 1)
-            sent[0][3].start()
+            advance(bulk, bulk + 1)
         wait_edges(s, 0)
 
         def two(i, acc, s=s):
@@ -382,9 +392,8 @@
         send_edges(s + 1, 0)
         settle(s)
         if s == 4:
-            for moves in sent:
-                for copy in moves:
-                    copy.wait_send()
+            for copy in queue[-flying:]:
+                copy.wait_send()
         if s == 6:
             loop(sections, lambda d: late_arrival(d).wait_recv())
             loop(sections, lambda d: late_sends(d).wait_send())

time: 63.8 us -> 62.2 us (0.975)
  Pallas kernels: 61.2 us -> 59.5 us
    pallas_call x1, Pallas kernels: 59.3 us -> 57.6 us  [on_device(): pl.pallas_call(functools.partial(kernel, sections, planes, rows), out_sha...]
where the time goes in v6:
time: 62.2 us; the launch traced here: 62 us
  Pallas kernels  59.5 us (96%)
  between operations  2.45 us (4%)
    pallas_call x1, Pallas kernels, on_device(): pl.pallas_call(functools.partial(kernel, sections, planes, rows), out_sha...  57.6 us
    pallas_call x1, Pallas kernels, on_device(): pl.pallas_call(finish_kernel, out_shape=(jax.ShapeDtypeStruct(chi_final.s...  1.88 us

profile of v6, /device:TPU:0, one launch (start us, length us, event | category | flops | bytes accessed | tf_op | source)
XLA Modules:
  0.0 62.0 jit_solution(10434284689225305054)
XLA Ops:
  0.6 57.6 %shard_map.76 = (f32[2,4,64,256]{3,2,1,0:T(8,128)}, f32[2,32,256]{2,1,0:T(8,128)}, f32[1]{0:T(128)}) custom-call(f32[2,4,64,256]{3,2,1,0:T(8,128)} %chi.1, f32[2,4,64,256]{3,2,1,0:T(8,128)} %psi_late.1, f32[2,4,64,256]{3,2,1,0:T(8,128)} %psi_early.1, f32[4,64,256]{2,1,0:T(8,128)} %trap.1, f32[2,32,256]{2,1,0:T(8,128)} %controls.1), custom_call_target="tpu_custom_call" | custom-call | flops 26214400 | bytes 3000000 | tf_op jit(solution)/shard_map/pallas_call | solution.py:520
  58.3 1.9 %shard_map.77 = (f32[2,4,64,256]{3,2,1,0:T(8,128)}, f32[2,32,256]{2,1,0:T(8,128)}) custom-call(f32[2,4,64,256]{3,2,1,0:T(8,128)} %get-tuple-element.8.field_in, f32[2,32,256]{2,1,0:T(8,128)} %get-tuple-element.9.grad_in), custom_call_target="tpu_custom_call" | custom-call | tf_op jit(solution)/shard_map/pallas_call | solution.py:565

commit v7 on v6

--- a/solution.py
+++ b/solution.py
@@ -105,7 +105,7 @@
         queue += [sent[i][1], sent[i][2]]
     queue += [sent[i][3] for i in range(planes)]
     bulk = len(queue) - planes
-    flying = 3
+    flying = 2
     for copy in queue[:flying]:
         copy.start()
 

time: 62.2 us -> 61.8 us (level)
  no operation moved by 1% of the time
where the time goes in v7:
time: 61.8 us; the launch traced here: 61.6 us
  Pallas kernels  59.1 us (96%)
  between operations  2.45 us (4%)
    pallas_call x1, Pallas kernels, on_device(): pl.pallas_call(functools.partial(kernel, sections, planes, rows), out_sha...  57.3 us
    pallas_call x1, Pallas kernels, on_device(): pl.pallas_call(finish_kernel, out_shape=(jax.ShapeDtypeStruct(chi_final.s...  1.88 us

profile of v7, /device:TPU:0, one launch (start us, length us, event | category | flops | bytes accessed | tf_op | source)
XLA Modules:
  0.0 61.6 jit_solution(12199187868752895695)
XLA Ops:
  0.6 57.3 %shard_map.76 = (f32[2,4,64,256]{3,2,1,0:T(8,128)}, f32[2,32,256]{2,1,0:T(8,128)}, f32[1]{0:T(128)}) custom-call(f32[2,4,64,256]{3,2,1,0:T(8,128)} %chi.1, f32[2,4,64,256]{3,2,1,0:T(8,128)} %psi_late.1, f32[2,4,64,256]{3,2,1,0:T(8,128)} %psi_early.1, f32[4,64,256]{2,1,0:T(8,128)} %trap.1, f32[2,32,256]{2,1,0:T(8,128)} %controls.1), custom_call_target="tpu_custom_call" | custom-call | flops 26214400 | bytes 3000000 | tf_op jit(solution)/shard_map/pallas_call | solution.py:520
  57.9 1.9 %shard_map.77 = (f32[2,4,64,256]{3,2,1,0:T(8,128)}, f32[2,32,256]{2,1,0:T(8,128)}) custom-call(f32[2,4,64,256]{3,2,1,0:T(8,128)} %get-tuple-element.8.field_in, f32[2,32,256]{2,1,0:T(8,128)} %get-tuple-element.9.grad_in), custom_call_target="tpu_custom_call" | custom-call | tf_op jit(solution)/shard_map/pallas_call | solution.py:565
